TPU v7x, 256 devices: a whole 4x4x8 slice. The times are simulated.
256 devices in a mesh: dp: 16 (over z_hi, y), block: 16 (over z_lo, x, core).
Axes of the slice: x: 4, y: 4, z: 8 (z_hi: 4, z_lo: 2; z = z_hi * 2 + z_lo), core: 2. Of those that a mesh axis runs over, the one named last changes fastest.
Arguments:
- acts: bfloat16 [4096, 4608], P('dp', 'block'), may hold values from -6 to 6
- cotan: bfloat16 [4096, 32768], P('dp', 'block'), may hold values from -0.125 to 0.125
- sketch_basis: bfloat16 [16, 16, 256, 4608], P('block', 'dp'), may hold values from -0.09375 to 0.09375
- sketch_values: float32 [16, 16, 256], P('block', 'dp'), may hold values from 500 to 20000
- start_basis: bfloat16 [16, 16, 256, 4608], P('block', 'dp'), may hold values from -6 to 6
Outputs:
- new_basis: bfloat16 [16, 16, 256, 4608], P('block', 'dp')
- new_values: float32 [16, 16, 256], P('block', 'dp')
- update: bfloat16 [4608, 32768], P('dp', 'block')
All inputs are finite; a program needn't handle non-finite values.
Results may differ from a plain program's by a relative error of at most 0.04.
Values may be sent and summed in bfloat16 or wider, within the bound.
A program may use at most 128 MiB of HBM per device.

v0:
```python
import jax
import jax.numpy as jnp
from jax import lax
from jax.sharding import PartitionSpec as P

ITERS = 2


epsilon = 1e-05


def sketch_block(grad_sum, basis, values, start_basis):
    grad_low = grad_sum.astype(jnp.bfloat16)
    scaled = (jnp.sqrt(values)[:, None] * basis.astype(jnp.float32)).astype(jnp.bfloat16)
    stacked = jnp.concatenate([scaled, grad_low], axis=0)
    rank_rows = basis.shape[0]
    basis_now = start_basis
    for sweep in range(ITERS):
        coords = lax.dot_general(
            basis_now, stacked, (((1,), (1,)), ((), ())), preferred_element_type=jnp.float32
        ).astype(jnp.bfloat16)
        images = jnp.dot(coords, stacked, preferred_element_type=jnp.float32)
        gram_matrix = jnp.dot(images, images.T, precision=lax.Precision.HIGHEST)
        factor = jnp.linalg.cholesky(gram_matrix)
        basis_now = lax.linalg.triangular_solve(factor, images, left_side=True, lower=True).astype(
            jnp.bfloat16
        )
    final = lax.dot_general(
        basis_now, stacked, (((1,), (1,)), ((), ())), preferred_element_type=jnp.float32
    )
    energy = jnp.sum(final * final, axis=1)
    lowest = jnp.min(energy)
    new_values = energy - lowest
    shrink = ((lowest + epsilon) / energy) ** 0.25 - 1.0
    weights = (shrink[:, None] * final[:, rank_rows:]).astype(jnp.bfloat16)
    return (basis_now, new_values, grad_low, weights)


def per_device(acts, cotan, sketch_basis, sketch_values, start_basis):
    gathered = lax.all_gather(acts, "block", axis=1, tiled=True)
    owners = lax.axis_size("dp")
    block_width = cotan.shape[1] // owners
    grad_sum = lax.psum_scatter(
        lax.dot_general(
            cotan, gathered, (((0,), (0,)), ((), ())), preferred_element_type=jnp.float32
        ).astype(jnp.bfloat16),
        "dp",
        scatter_dimension=0,
        tiled=True,
    ).astype(jnp.float32)
    basis_now, new_values, grad_low, weights = sketch_block(
        grad_sum, sketch_basis[0, 0], sketch_values[0, 0], start_basis[0, 0]
    )
    rank_rows = basis_now.shape[0]
    joined = jnp.concatenate([grad_low, basis_now], axis=0)
    received = lax.all_to_all(joined, "dp", split_axis=1, concat_axis=0, tiled=True)
    row_count = received.shape[1]
    received = received.reshape(owners, block_width + rank_rows, row_count)
    grad_rows = received[:, :block_width]
    basis_rows = received[:, block_width:]
    coef_all = lax.all_gather(weights, "dp", axis=0, tiled=True).reshape(
        owners, rank_rows, block_width
    )
    projected = jnp.einsum("kjr,kjc->rkc", basis_rows, coef_all, preferred_element_type=jnp.float32)
    update = projected + jnp.transpose(grad_rows, (2, 0, 1)).astype(jnp.float32)
    update = update.reshape(row_count, owners * block_width).astype(jnp.bfloat16)
    return (basis_now[None, None], new_values[None, None], update)


def solution(mesh):
    return jax.shard_map(
        per_device,
        mesh=mesh,
        in_specs=(
            P("dp", "block"),
            P("dp", "block"),
            P("block", "dp", None, None),
            P("block", "dp", None),
            P("block", "dp", None, None),
        ),
        out_specs=(P("block", "dp", None, None), P("block", "dp", None), P("dp", "block")),
        check_vma=False,
    )
```

profile of v0, /device:TPU:26, one launch (start us, length us, event | category | flops | bytes accessed | tf_op | source)
XLA Modules:
  0.0 605.9 jit_solution(70497343774400709)
XLA Ops:
  8.0 41.3 %all-gather.3.cloned.1.call-done = bf16[256,4608]{0,1:T(8,128)(2,1)} async-done(((bf16[256,288]{0,1:T(8,128)(2,1)}), bf16[256,4608]{0,1:T(8,128)(2,1)}) %all-gather.3.cloned.1.call-update) | async-done | bytes 2359312 | tf_op jit(solution)/shard_map/all_gather | solution.py:40
  49.3 10.7 %convolution_convert_fusion = bf16[2048,4608]{1,0:T(8,128)(2,1)} fusion(bf16[256,2048]{1,0:T(8,128)(2,1)} %param.9, bf16[256,4608]{0,1:T(8,128)(2,1)} %all-gather.3.cloned.1.call-done), kind=kOutput, calls=%fused_computation.4 | convolution fusion | flops 4841275392 | bytes 22282240 | tf_op jit(solution)/shard_map/dot_general | solution.py:44
  60.7 3.6 fusion
  64.3 224.1 %reduce-scatter.2.cloned.1.call-done = bf16[128,4608]{1,0:T(8,128)(2,1)} async-done(((bf16[2048,4608]{1,0:T(8,128)(2,1)}), bf16[128,4608]{1,0:T(8,128)(2,1)}) %reduce-scatter.2.cloned.1.call-update) | async-done | bytes 1179664 | tf_op jit(solution)/shard_map/reduce_scatter | solution.py:43
  288.4 9.5 %fusion.21 = f32[256,4608]{1,0:T(8,128)} fusion(bf16[1,1,256,4608]{3,2,1,0:T(8,128)(2,1)S(1)} %copy-done, bf16[128,4608]{1,0:T(8,128)(2,1)} %reduce-scatter.2.cloned.1.call-done, bf16[256,4608]{1,0:T(8,128)(2,1)} %fusion), kind=kOutput, calls=%fused_computation.28 | convolution fusion | flops 1826193408 | bytes 10616832 | tf_op jit(solution)/shard_map/dot_general | solution.py:22
  297.9 13.4 %fusion.50 = f32[256,256]{1,0:T(8,128)S(1)} fusion(f32[256,4608]{1,0:T(8,128)} %fusion.21), kind=kOutput, calls=%fused_computation.83 | convolution fusion | flops 3623878656 | bytes 4980736 | tf_op jit(solution)/shard_map/dot_general | solution.py:23
  311.5 11.7 %cholesky.130 = f32[128,128]{1,0:T(8,128)S(1)} custom-call(f32[128,128]{1,0:T(8,128)S(1)} %cholesky.194), custom_call_target="Cholesky" | custom-call | tf_op jit(solution)/shard_map/jit(cholesky)/cholesky | solution.py:24
  323.2 9.8 %custom-call.13 = f32[1,128,128]{1,2,0:T(8,128)S(1)} custom-call(f32[1,128,128]{2,1,0:T(8,128)S(1)} %get-tuple-element.48), custom_call_target="InvertDiagBlocksLowerTriangular" | custom-call | tf_op jit(solution)/shard_map/jit(cholesky)/cholesky | solution.py:24
  333.6 11.7 %cholesky.147 = f32[128,128]{1,0:T(8,128)S(1)} custom-call(f32[128,128]{1,0:T(8,128)S(1)} %convolution_subtract_fusion.3), custom_call_target="Cholesky" | custom-call | tf_op jit(solution)/shard_map/jit(cholesky)/cholesky | solution.py:24
  347.4 4.0 while.4
  351.4 19.9 %custom-call.14 = f32[2,128,128]{1,2,0:T(8,128)S(1)} custom-call(f32[2,128,128]{2,1,0:T(8,128)S(1)} %get-tuple-element.19), custom_call_target="InvertDiagBlocksLowerTriangular" | custom-call | tf_op jit(solution)/shard_map/triangular_solve/custom-call.0 | solution.py:25
  371.3 3.9 fusion.6
  375.3 2.2 convolution_subtract_fusion.1
  377.5 4.1 fusion.32
  381.6 7.6 %fusion.19 = f32[256,4608]{1,0:T(8,128)} fusion(bf16[128,4608]{1,0:T(8,128)(2,1)} %fusion.32, f32[128,4608]{1,0:T(8,128)S(1)} %fusion.6, bf16[128,4608]{1,0:T(8,128)(2,1)S(1)} %copy-done.5, bf16[256,4608]{1,0:T(8,128)(2,1)} %fusion), kind=kOutput, calls=%fused_computation.27 | convolution fusion | flops 1830912000 | bytes 11796480 | tf_op jit(solution)/shard_map/dot_general | solution.py:22
  389.2 13.6 %fusion.51 = f32[256,256]{1,0:T(8,128)S(1)} fusion(f32[256,4608]{1,0:T(8,128)} %fusion.19), kind=kOutput, calls=%fused_computation.84 | convolution fusion | flops 3623878656 | bytes 4980736 | tf_op jit(solution)/shard_map/dot_general | solution.py:23
  403.0 11.7 %cholesky.164 = f32[128,128]{1,0:T(8,128)S(1)} custom-call(f32[128,128]{1,0:T(8,128)S(1)} %cholesky.197), custom_call_target="Cholesky" | custom-call | tf_op jit(solution)/shard_map/jit(cholesky)/cholesky | solution.py:24
  414.7 9.8 %custom-call.15 = f32[1,128,128]{1,2,0:T(8,128)S(1)} custom-call(f32[1,128,128]{2,1,0:T(8,128)S(1)} %get-tuple-element.44), custom_call_target="InvertDiagBlocksLowerTriangular" | custom-call | tf_op jit(solution)/shard_map/jit(cholesky)/cholesky | solution.py:24
  425.0 11.7 %cholesky.181 = f32[128,128]{1,0:T(8,128)S(1)} custom-call(f32[128,128]{1,0:T(8,128)S(1)} %convolution_subtract_fusion.2), custom_call_target="Cholesky" | custom-call | tf_op jit(solution)/shard_map/jit(cholesky)/cholesky | solution.py:24
  439.5 4.1 while.5
  443.6 19.8 %custom-call.16 = f32[2,128,128]{1,2,0:T(8,128)S(1)} custom-call(f32[2,128,128]{2,1,0:T(8,128)S(1)} %get-tuple-element.20), custom_call_target="InvertDiagBlocksLowerTriangular" | custom-call | tf_op jit(solution)/shard_map/triangular_solve/custom-call.0 | solution.py:25
  463.4 3.9 fusion.4
  467.4 2.2 convolution_subtract_fusion
  469.6 3.0 fusion.28
  474.3 2.0 pad_maximum_fusion.1
  476.3 5.7 copy.13
  482.1 6.9 %all-to-all-start = ((bf16[384,16,288]{0,2,1:T(8,128)(2,1)}), bf16[384,16,288]{0,2,1:T(8,128)(2,1)}, u32[]{:S(2)}, u32[]{:S(2)}) async-start(bf16[384,16,288]{0,2,1:T(8,128)(2,1)} %bitcast.93), calls=%async_computation.1 | async-start | bytes 7077888 | tf_op jit(solution)/shard_map/all_to_all | solution.py:56
  489.0 4.9 multiply_reduce_fusion
  496.3 1.6 fusion.26
  498.0 1.6 fusion.68
  499.6 95.1 %all-gather.5.cloned.1.call-done = bf16[4096,128]{1,0:T(8,128)(2,1)} async-done(((bf16[256,128]{1,0:T(8,128)(2,1)}), bf16[4096,128]{1,0:T(8,128)(2,1)}) %all-gather.5.cloned.1.call-update) | async-done | bytes 1048592 | tf_op jit(solution)/shard_map/all_gather | solution.py:61
  594.7 3.2 fusion.12
  (69 shorter events, 17.9 us)
Async XLA Ops:
  7.2 281.2 %copy-start = (bf16[1,1,256,4608]{3,2,1,0:T(8,128)(2,1)S(1)}, bf16[1,1,256,4608]{3,2,1,0:T(8,128)(2,1)}, u32[]{:S(2)}) copy-start(bf16[1,1,256,4608]{3,2,1,0:T(8,128)(2,1)} %param.12) | copy-start | bytes 7077892
  7.2 42.1 %all-gather.3.cloned.1.call-start = ((), (), s32[]{:S(2)}) async-start(), calls=%async_computation.2 | async-start | bytes 2506752 | tf_op jit(solution)/shard_map/all_gather | solution.py:40
  7.9 280.5 %reduce-scatter.2.cloned.1.call-start = ((), (), s32[]{:S(2)}) async-start(), calls=%async_computation.3 | async-start | bytes 20054016 | tf_op jit(solution)/shard_map/reduce_scatter | solution.py:43
  60.0 0.7 copy-start.9
  371.3 4.0 copy-start.7
  371.3 4.0 copy-start.3
  377.5 4.1 copy-start.5
  463.4 4.0 copy-start.8
  463.4 4.0 copy-start.2
  472.6 1.7 copy-start.6
  472.8 1.5 copy-start.4
  482.1 112.6 %all-to-all-start = ((bf16[384,16,288]{0,2,1:T(8,128)(2,1)}), bf16[384,16,288]{0,2,1:T(8,128)(2,1)}, u32[]{:S(2)}, u32[]{:S(2)}) async-start(bf16[384,16,288]{0,2,1:T(8,128)(2,1)} %bitcast.93), calls=%async_computation.1 | async-start | bytes 7077888 | tf_op jit(solution)/shard_map/all_to_all | solution.py:56
  488.9 105.7 %all-gather.5.cloned.1.call-start = ((), (), s32[]{:S(2)}) async-start(), calls=%async_computation.4 | async-start | bytes 1114112 | tf_op jit(solution)/shard_map/all_gather | solution.py:61
  594.6 4.6 copy-start.1
Sparse Core Ops, SparseCore 0:
  9.9 39.3 all-gather.2
  60.2 228.1 reduce-scatter.1
  498.1 96.4 all-gather.4
where the time goes:
time: 616 us; the launch traced here: 606 us
  waiting for transfers between devices  361 us (59%)
  other arithmetic  119 us (19%)
  matrix products  83.2 us (14%)
  local copies, waits for them, and re-layouts  17.6 us (3%)
  between operations  17.5 us (3%)
  starting transfers between devices  7 us (1%)
    reduce_scatter x1, waiting for transfers between devices, per_device(): lax.psum_scatter(lax.dot_general(cotan, gathered, (((0,), (0,)), ((), ())...  224 us
    all_gather x1, waiting for transfers between devices, per_device(): lax.all_gather(weights, 'dp', axis=0, tiled=True)  95.1 us
    another operation x13, other arithmetic, sketch_block(): factor = jnp.linalg.cholesky(gram_matrix)  68.6 us
    all_gather x1, waiting for transfers between devices, per_device(): gathered = lax.all_gather(acts, 'block', axis=1, tiled=True)  41.3 us
    another operation x5, other arithmetic, sketch_block(): lax.linalg.triangular_solve(factor, images, left_side=True, lower=True)  39.8 us
    dot_general x2, matrix products, sketch_block(): gram_matrix = jnp.dot(images, images.T, precision=lax.Precision.HIGHEST)  27 us
    another operation x6, matrix products, sketch_block(): lax.linalg.triangular_solve(factor, images, left_side=True, lower=True)  19.4 us
    dot_general x2, matrix products, sketch_block(): images = jnp.dot(coords, stacked, preferred_element_type=jnp.float32)  17.1 us
  transfers between devices with their start and end apart: 4, of which 3 were waited for; matrix products, arithmetic and copies ran while one was open for 2% of the time, Pallas kernels for 0%

commit v1 on v0

v1 whole, which is shorter than its diff:
```python
import functools

import jax
import jax.numpy as jnp
from jax import lax
from jax.experimental import pallas as pl
from jax.experimental.pallas import tpu as pltpu
from jax.sharding import PartitionSpec as P

HIGH = lax.Precision.HIGHEST
F32, BF = jnp.float32, jnp.bfloat16
EPSILON = 1e-05
MESH = pl.DeviceIdType.MESH
PANEL = 8


def mm(a, b, ca, cb, precision=None):
    return lax.dot_general(
        a, b, (((ca,), (cb,)), ((), ())), precision=precision, preferred_element_type=F32
    )


def split(value, parts=3):
    out = []
    for _ in range(parts):
        out.append(value.astype(BF))
        value = value - out[-1].astype(F32)
    return out


def inverse_factor(block):
    n = block.shape[0]
    count = n // 8
    rows = [block[8 * i : 8 * i + 8, :] for i in range(count)]
    lane = lax.broadcasted_iota(jnp.int32, (8, n), 1)
    sub = lax.broadcasted_iota(jnp.int32, (8, n), 0)

    def full(v):
        return jnp.broadcast_to(v, (8, n))

    for start in range(0, n, PANEL):
        first = start // 8
        cols = [
            {i: full(rows[i][:, start + q : start + q + 1]) for i in range(first, count)}
            for q in range(PANEL)
        ]
        for q in range(PANEL):
            j = start + q
            b, r = divmod(j, 8)
            recip = 1.0 / full(cols[q][b][r : r + 1, :])
            mine = {i: cols[q][i] for i in range(b, count)}
            if r == 7:
                del mine[b]
            else:
                mine[b] = jnp.where(sub > r, mine[b], 0.0)
            mine = {i: m * recip for i, m in mine.items()}
            for k in range(q + 1, PANEL):
                pivot = full(cols[k][b][r : r + 1, :])
                for i, m in mine.items():
                    cols[k][i] = cols[k][i] - m * pivot
            here = lane == j
            row = jnp.where(here, 1.0, full(rows[b][r : r + 1, :]))
            for i, m in mine.items():
                gone = here & (sub > r) if i == b else here
                rows[i] = jnp.where(gone, 0.0, rows[i]) - m * row
    m = jnp.concatenate(rows, axis=0)
    ln = lax.broadcasted_iota(jnp.int32, (n, n), 1)
    sb = lax.broadcasted_iota(jnp.int32, (n, n), 0)
    diag = jnp.sum(jnp.where(ln == sb, m, 0.0), axis=1, keepdims=True)
    low = jnp.where(sb > ln, m, jnp.where(sb == ln, 1.0, 0.0))
    return low * lax.rsqrt(diag)


def solver(gram):
    h = gram.shape[0] // 2
    top = inverse_factor(gram[:h, :h])
    side = mm(gram[h:, :h], top, 1, 1, HIGH)
    low = inverse_factor(gram[h:, h:] - mm(side, side, 1, 1, HIGH))

    def solve(x):
        head = mm(top, x[:h], 1, 0, HIGH)
        tail = mm(low, x[h:] - mm(side, head, 1, 0, HIGH), 1, 0, HIGH)
        return jnp.concatenate([head, tail], axis=0)

    return solve


def sketch_kernel(grad_ref, basis_ref, values_ref, start_ref, new_ref, energy_ref, update_ref, scaled_ref):
    rank, depth = basis_ref.shape
    width = grad_ref.shape[1]
    step = 512
    eye = lax.broadcasted_iota(jnp.int32, (rank, rank), 0) == lax.broadcasted_iota(
        jnp.int32, (rank, rank), 1
    )
    root = jnp.sqrt(jnp.sum(jnp.where(eye, values_ref[...], 0.0), axis=1, keepdims=True))

    gram_bb = jnp.zeros((rank, rank), F32)
    coord_b = jnp.zeros((rank, rank), F32)
    gram_bg = jnp.zeros((rank, width), F32)
    coord_g = jnp.zeros((rank, width), F32)
    gram_gg = jnp.zeros((width, width), F32)
    for at in range(0, depth, step):
        cut = slice(at, at + step)
        scaled = (root * basis_ref[:, cut].astype(F32)).astype(BF)
        scaled_ref[:, cut] = scaled
        start = start_ref[:, cut]
        grad = grad_ref[cut, :]
        gram_bb += mm(scaled, scaled, 1, 1)
        coord_b += mm(start, scaled, 1, 1)
        gram_bg += mm(scaled, grad, 1, 0)
        coord_g += mm(start, grad, 1, 0)
        gram_gg += mm(grad, grad, 0, 0)
    gram = jnp.concatenate(
        [
            jnp.concatenate([gram_bb, gram_bg], axis=1),
            jnp.concatenate([gram_bg.T, gram_gg], axis=1),
        ],
        axis=0,
    )
    gram_parts = split(gram)

    def sweep(coords):
        mapped = sum(mm(coords, part, 1, 0) for part in gram_parts)
        images_gram = sum(mm(part, coords, 1, 1) for part in split(mapped))
        return mapped, solver(images_gram)

    coords = jnp.concatenate([coord_b, coord_g], axis=1).astype(BF)
    mapped, solve = sweep(coords)
    coords = solve(mapped).astype(BF)
    mapped, solve = sweep(coords)
    total = coords.shape[1]
    solved = solve(jnp.concatenate([coords.astype(F32), mapped], axis=1))
    combine = split(solved[:, :total])
    final = solved[:, total:]
    square = final * final
    energy = jnp.sum(square, axis=1, keepdims=True)
    lowest = jnp.min(energy)
    energy_row = jnp.sum(jnp.where(eye, energy, 0.0), axis=0, keepdims=True)
    energy_ref[...] = energy_row - lowest
    shrink = jnp.sqrt(jnp.sqrt((lowest + EPSILON) / energy)) - 1.0
    weights = (shrink * final[:, rank:]).astype(BF)
    for at in range(0, depth, step):
        cut = slice(at, at + step)
        grad = grad_ref[cut, :]
        scaled = scaled_ref[:, cut]
        basis = sum(mm(part[:, :rank], scaled, 1, 0) for part in combine)
        basis += sum(mm(part[:, rank:], grad, 1, 1) for part in combine)
        basis = basis.astype(BF)
        new_ref[:, cut] = basis
        update_ref[cut, :] = (grad.astype(F32) + mm(basis, weights, 0, 0)).astype(BF)


def sketch(grad, basis, values, start):
    rank, depth = basis.shape
    width = grad.shape[1]
    vmem = pl.BlockSpec(memory_space=pltpu.VMEM)
    return pl.pallas_call(
        sketch_kernel,
        out_shape=(
            jax.ShapeDtypeStruct((rank, depth), BF),
            jax.ShapeDtypeStruct((1, rank), F32),
            jax.ShapeDtypeStruct((depth, width), BF),
        ),
        in_specs=[vmem] * 4,
        out_specs=(vmem, vmem, vmem),
        scratch_shapes=[pltpu.VMEM((rank, depth), BF)],
        compiler_params=pltpu.CompilerParams(vmem_limit_bytes=48 << 20),
    )(grad, basis, values, start)


def exchange_kernel(shares, update_ref, out_ref, own_sem, send_sem, recv_sem):
    zh, y = lax.axis_index("zh"), lax.axis_index("y")
    ys = lax.axis_size("y")
    me = zh * ys + y
    rows, width = out_ref.shape[0], update_ref.shape[1]
    peers = [lax.rem(me + r, shares) for r in range(shares)]

    barrier = pltpu.get_barrier_semaphore()
    for peer in peers[1:]:
        pl.semaphore_signal(
            barrier, inc=1, device_id={"zh": peer // ys, "y": lax.rem(peer, ys)}, device_id_type=MESH
        )
    pl.semaphore_wait(barrier, shares - 1)

    columns = out_ref.at[:, pl.ds(pl.multiple_of(me * width, width), width)]

    def piece(peer):
        return update_ref.at[pl.ds(pl.multiple_of(peer * rows, 16), rows), :]

    copies = []
    for r in range(1, shares):
        peer = peers[r]
        copy = pltpu.make_async_remote_copy(
            src_ref=piece(peer),
            dst_ref=columns,
            send_sem=send_sem.at[r],
            recv_sem=recv_sem.at[r],
            device_id={"zh": peer // ys, "y": lax.rem(peer, ys)},
            device_id_type=MESH,
        )
        copy.start()
        copies.append(copy)
    own = pltpu.make_async_copy(piece(me), columns, own_sem)
    own.start()
    own.wait()
    for copy in copies:
        copy.wait()


def exchange(update, shares):
    depth, width = update.shape
    anywhere = pl.BlockSpec(memory_space=pl.ANY)
    return pl.pallas_call(
        functools.partial(exchange_kernel, shares),
        out_shape=jax.ShapeDtypeStruct((depth // shares, width * shares), BF),
        in_specs=[anywhere],
        out_specs=anywhere,
        scratch_shapes=[
            pltpu.SemaphoreType.DMA,
            pltpu.SemaphoreType.DMA((shares,)),
            pltpu.SemaphoreType.DMA((shares,)),
        ],
        compiler_params=pltpu.CompilerParams(collective_id=1, has_side_effects=True),
    )(update)


def per_device(acts, cotan, sketch_basis, sketch_values, start_basis):
    gathered = lax.all_gather(acts, ("zl", "x", "c"), axis=1, tiled=True)
    shares = lax.axis_size("zh") * lax.axis_size("y")
    grad = lax.psum_scatter(
        lax.dot_general(
            cotan, gathered, (((0,), (0,)), ((), ())), preferred_element_type=F32
        ).astype(BF),
        ("zh", "y"),
        scatter_dimension=0,
        tiled=True,
    ).T
    basis, values, update = sketch(grad, sketch_basis[0, 0], sketch_values[0], start_basis[0, 0])
    update = exchange(update, shares)
    return basis[None, None], values[None], update


def solution(mesh):
    fine = jax.sharding.Mesh(mesh.devices.reshape(4, 4, 2, 4, 2), ("zh", "y", "zl", "x", "c"))
    dp, block = ("zh", "y"), ("zl", "x", "c")
    return jax.shard_map(
        per_device,
        mesh=fine,
        in_specs=(
            P(dp, block),
            P(dp, block),
            P(block, dp, None, None),
            P(block, dp, None),
            P(block, dp, None, None),
        ),
        out_specs=(P(block, dp, None, None), P(block, dp, None), P(dp, block)),
        check_vma=False,
    )
```

time: 616 us -> 375 us (0.61); the launches traced: 606 us -> 375 us
  other arithmetic: 119 us -> 0 us
  waiting for transfers between devices: 361 us -> 270 us
  Pallas kernels: 0 us -> 73 us
  matrix products: 83.2 us -> 10.8 us
  local copies, waits for them, and re-layouts: 17.6 us -> 7.04 us
  starting transfers between devices: 7 us -> 0.08 us
    unnamed x3, waiting for transfers between devices: 0.71 us -> 229 us
    reduce_scatter x1 -> x0, waiting for transfers between devices: 224 us -> none  [per_device(): lax.psum_scatter(lax.dot_general(cotan, gathered, (((0,), (0,)), ((), ())...]
    another operation x18 -> x0, other arithmetic: 108 us -> none  [the longest x13 68.6 us: sketch_block(): factor = jnp.linalg.cholesky(gram_matrix)]
    all_gather x2 -> x1, waiting for transfers between devices: 136 us -> 41.3 us  [per_device(): gathered = lax.all_gather(acts, ('zl', 'x', 'c'), axis=1, tiled=True)]
    pallas_call x0 -> x2, Pallas kernels: none -> 73 us  [the longest x1 37.9 us: exchange(): pl.pallas_call(functools.partial(exchange_kernel, shares), out_shape=jax....]
    dot_general x6 -> x0, matrix products: 52.2 us -> none  [the longest x2 27 us: sketch_block(): gram_matrix = jnp.dot(images, images.T, precision=lax.Precision.HIGHEST)]
    another operation x10 -> x0, matrix products: 20.3 us -> none  [the longest x6 19.4 us: sketch_block(): lax.linalg.triangular_solve(factor, images, left_side=True, lower=True)]
    another operation x19 -> x0, local copies, waits for them, and re-layouts: 8.09 us -> none  [the longest x15 8.04 us: sketch_block(): lax.linalg.triangular_solve(factor, images, left_side=True, lower=True)]
  transfers between devices with their start and end apart: 4 -> 2, of which waited for: 3 -> 2; matrix products, arithmetic and copies ran while one was open for 2% -> 0% of each run, Pallas kernels for 0% -> 0%
where the time goes in v1:
time: 375 us
  waiting for transfers between devices  270 us (72%)
  Pallas kernels  73 us (19%)
  between operations  14.1 us (4%)
  matrix products  10.8 us (3%)
  local copies, waits for them, and re-layouts  7.04 us (2%)
    unnamed x3, waiting for transfers between devices  229 us
    all_gather x1, waiting for transfers between devices, per_device(): gathered = lax.all_gather(acts, ('zl', 'x', 'c'), axis=1, tiled=True)  41.3 us
    pallas_call x1, Pallas kernels, exchange(): pl.pallas_call(functools.partial(exchange_kernel, shares), out_shape=jax....  37.9 us
    pallas_call x1, Pallas kernels, sketch(): pl.pallas_call(sketch_kernel, out_shape=(jax.ShapeDtypeStruct((rank, dept...  35.1 us
    dot_general x1, matrix products, per_device(): lax.dot_general(cotan, gathered, (((0,), (0,)), ((), ())), preferred_elem...  10.8 us
  transfers between devices with their start and end apart: 2, of which 2 were waited for; matrix products, arithmetic and copies ran while one was open for 0% of the time, Pallas kernels for 0%

profile of v1, /device:TPU:26, one launch (start us, length us, event | category | flops | bytes accessed | tf_op | source)
XLA Modules:
  0.0 375.3 jit_solution(4786180971917148594)
XLA Ops:
  7.2 0.0 copy-start
  7.2 0.0 all-gather.2.cloned.1.call-start
  7.2 0.7 all-gather.2.cloned.1.call-update
  7.9 0.0 reduce-scatter.4.cloned.1.call-start
  8.0 41.3 %all-gather.2.cloned.1.call-done = bf16[256,4608]{0,1:T(8,128)(2,1)} async-done(((bf16[256,288]{0,1:T(8,128)(2,1)}), bf16[256,4608]{0,1:T(8,128)(2,1)}) %all-gather.2.cloned.1.call-update) | async-done | bytes 2359312 | tf_op jit(solution)/shard_map/all_gather | solution.py:228
  49.3 0.0 copy-done
  49.3 10.8 %convolution_convert_fusion = bf16[2048,4608]{1,0:T(8,128)(2,1)} fusion(bf16[256,2048]{1,0:T(8,128)(2,1)S(1)} %copy-done, bf16[256,4608]{0,1:T(8,128)(2,1)} %all-gather.2.cloned.1.call-done), kind=kOutput, calls=%fused_computation | convolution fusion | flops 4841275392 | bytes 22282240 | tf_op jit(solution)/shard_map/dot_general | solution.py:231
  60.1 0.0 reduce-scatter.4.cloned.1.call-update
  60.2 0.0 copy-start.3
  60.2 228.2 %reduce-scatter.4.cloned.1.call-done = bf16[128,4608]{1,0:T(8,128)(2,1)} async-done(((bf16[2048,4608]{1,0:T(8,128)(2,1)}), bf16[128,4608]{1,0:T(8,128)(2,1)}) %reduce-scatter.4.cloned.1.call-update) | async-done | bytes 1179664
  288.3 1.9 copy.11
  290.3 0.0 copy-done.3
  290.3 0.0 copy-start.1
  290.3 1.7 copy-done.1
  292.0 35.1 %shard_map.76 = (bf16[256,4608]{1,0:T(8,128)(2,1)}, f32[1,256]{1,0:T(1,128)}, bf16[4608,128]{1,0:T(8,128)(2,1)S(1)}) custom-call(bf16[4608,128]{1,0:T(8,128)(2,1)S(1)} %bitcast.9, bf16[256,4608]{1,0:T(8,128)(2,1)S(1)} %bitcast.10, f32[1,256]{1,0:T(1,128)S(1)} %bitcast.11, bf16[256,4608]{1,0:T(8,128)(2,1)} %bitcast.12), custom_call_target="tpu_custom_call" | custom-call | tf_op jit(solution)/shard_map/pallas_call | solution.py:157
  327.1 0.0 copy-start.2
  327.1 1.0 copy-done.2
  328.1 37.9 %shard_map.77 = bf16[288,2048]{1,0:T(8,128)(2,1)} custom-call(bf16[4608,128]{1,0:T(8,128)(2,1)} %copy-done.2), custom_call_target="tpu_custom_call" | custom-call | tf_op jit(solution)/shard_map/pallas_call | solution.py:213
  366.0 2.4 copy.13
Async XLA Ops:
  7.2 42.1 %copy-start = (bf16[256,2048]{1,0:T(8,128)(2,1)S(1)}, bf16[256,2048]{1,0:T(8,128)(2,1)}, u32[]{:S(2)}) copy-start(bf16[256,2048]{1,0:T(8,128)(2,1)} %param.6) | copy-start | bytes 3145732
  7.2 42.1 %all-gather.2.cloned.1.call-start = ((), (), s32[]{:S(2)}) async-start(), calls=%async_computation.1 | async-start | bytes 2506752 | tf_op jit(solution)/shard_map/all_gather | solution.py:228
  7.9 280.4 %reduce-scatter.4.cloned.1.call-start = ((), (), s32[]{:S(2)}) async-start(), calls=%async_computation.2 | async-start | bytes 20054016
  60.2 230.1 %copy-start.3 = (f32[1,1,256]{2,1,0:T(1,128)S(1)}, f32[1,1,256]{2,1,0:T(1,128)}, u32[]{:S(2)}) copy-start(f32[1,1,256]{2,1,0:T(1,128)} %param.8) | copy-start | bytes 3076
  290.3 1.7 copy-start.1
  327.1 1.0 copy-start.2
Sparse Core Ops, SparseCore 0:
  9.9 39.3 all-gather.1
  60.3 228.0 reduce-scatter.3

commit v2 on v1

--- a/solution.py
+++ b/solution.py
@@ -224,17 +224,214 @@
     )(update)
 
 
+def gradient_kernel(
+    acts_ref, cotan_ref, out_ref, acts_all, cotan_all, total, sums,
+    own_sem, z_send, z_recv, y_send, y_recv, d_send, d_recv, x_send, x_recv, c_send, c_recv, g_send, g_recv,
+):
+    zh, y, zl, x, c = (lax.axis_index(name) for name in ("zh", "y", "zl", "x", "c"))
+    feats, tokens = acts_ref.shape
+    width = out_ref.shape[-1]
+
+    def ring(value, shift):
+        return lax.rem(value + shift, 4)
+
+    def remote(src, dst, send, recv, **where):
+        return pltpu.make_async_remote_copy(
+            src_ref=src, dst_ref=dst, send_sem=send, recv_sem=recv, device_id=where, device_id_type=MESH
+        )
+
+    barrier = pltpu.get_barrier_semaphore()
+    greeted = 0
+    for i in range(4):
+        for j in range(4):
+            if i or j:
+                pl.semaphore_signal(
+                    barrier, inc=1, device_id={"zh": ring(zh, i), "y": ring(y, j)}, device_id_type=MESH
+                )
+                greeted += 1
+        pl.semaphore_signal(
+            barrier, inc=1, device_id={"zh": ring(zh, i), "zl": 1 - zl}, device_id_type=MESH
+        )
+        greeted += 1
+        for flip in range(2):
+            if i or flip:
+                pl.semaphore_signal(
+                    barrier,
+                    inc=1,
+                    device_id={"x": ring(x, i), "c": lax.rem(c + flip, 2)},
+                    device_id_type=MESH,
+                )
+                greeted += 1
+    pl.semaphore_wait(barrier, greeted)
+
+    started = []
+
+    def go(copy):
+        copy.start()
+        started.append(copy)
+
+    def column(xx, cc):
+        return pl.ds(pl.multiple_of((xx * 2 + cc) * width, width), width)
+
+    mine = column(x, c)
+    order = (0, 1, 3, 2)
+
+    def z_copy(to_zh, to_zl):
+        return remote(
+            acts_ref, acts_all.at[y, zh, zl], z_send.at[to_zh * 2 + to_zl], z_recv.at[zh * 2 + zl],
+            zh=to_zh, zl=to_zl,
+        )
+
+    def d_copy(to_zh, to_y):
+        piece = pl.ds(pl.multiple_of((to_zh * 4 + to_y) * width, width), width)
+        return remote(
+            cotan_ref.at[:, piece], cotan_all.at[zh, y, :, mine],
+            d_send.at[to_zh * 4 + to_y], d_recv.at[zh * 4 + y], zh=to_zh, y=to_y,
+        )
+
+    for r in order:
+        if r:
+            go(z_copy(ring(zh, r), zl))
+        go(z_copy(ring(zh, r), 1 - zl))
+        for j in order:
+            if r or j:
+                go(d_copy(ring(zh, r), ring(y, j)))
+    own_acts = pltpu.make_async_copy(acts_ref, acts_all.at[y, zh, zl], own_sem.at[0])
+    own_acts.start()
+    piece = pl.ds(pl.multiple_of((zh * 4 + y) * width, width), width)
+    own_cotan = pltpu.make_async_copy(cotan_ref.at[:, piece], cotan_all.at[zh, y, :, mine], own_sem.at[1])
+    own_cotan.start()
+
+    def arrived(dst, sem):
+        remote(dst, dst, sem, sem, x=ring(x, 1)).wait_recv()
+
+    def first(t):
+        r = order[t]
+        src = ring(zh, r)
+        if r:
+            arrived(acts_all.at[y, src, zl], z_recv.at[src * 2 + zl])
+        else:
+            own_acts.wait()
+        arrived(acts_all.at[y, src, 1 - zl], z_recv.at[src * 2 + 1 - zl])
+        block = acts_all.at[y, src]
+        go(remote(block, block, y_send.at[0, src], y_recv.at[0, src], y=ring(y, 1)))
+        go(remote(block, block, y_send.at[1, src], y_recv.at[1, src], y=ring(y, 3)))
+        for j in range(4):
+            if r or j:
+                yy = ring(y, j)
+                arrived(cotan_all.at[src, yy, :, mine], d_recv.at[src * 4 + yy])
+            else:
+                own_cotan.wait()
+        block = cotan_all.at[src, :, :, mine]
+        go(remote(block, block, x_send.at[0, src], x_recv.at[0, src], x=ring(x, 1)))
+        go(remote(block, block, x_send.at[1, src], x_recv.at[1, src], x=ring(x, 3)))
+        go(remote(block, block, c_send.at[0, src], c_recv.at[0, src], c=1 - c))
+
+    def second(t):
+        src = ring(zh, order[t])
+        up = t % 2 == 0
+        for k, (shift, onward) in enumerate(((3, up), (1, not up))):
+            block = acts_all.at[ring(y, shift), src]
+            arrived(block, y_recv.at[k, src])
+            if onward:
+                go(remote(block, block, y_send.at[2, src], y_recv.at[2, src], y=ring(y, 4 - shift)))
+        for k, (shift, onward) in enumerate(((3, up), (1, not up))):
+            block = cotan_all.at[src, :, :, column(ring(x, shift), c)]
+            arrived(block, x_recv.at[k, src])
+            if onward:
+                go(remote(block, block, x_send.at[2, src], x_recv.at[2, src], x=ring(x, 4 - shift)))
+            go(remote(block, block, c_send.at[shift, src], c_recv.at[shift, src], c=1 - c))
+
+    def third(t):
+        src = ring(zh, order[t])
+        block = cotan_all.at[src, :, :, column(ring(x, 2), c)]
+        arrived(block, x_recv.at[2, src])
+        go(remote(block, block, c_send.at[2, src], c_recv.at[2, src], c=1 - c))
+        arrived(acts_all.at[ring(y, 2), src], y_recv.at[2, src])
+
+    def multiply(t):
+        src = ring(zh, order[t])
+        for shift in range(4):
+            arrived(cotan_all.at[src, :, :, column(ring(x, shift), 1 - c)], c_recv.at[shift, src])
+
+        def tile(n, carry):
+            cut = pl.ds(pl.multiple_of(n * 256, 256), 256)
+            part = jnp.zeros((2 * feats, 256), F32) if t == 0 else total[:, cut]
+            for j in range(4):
+                left = acts_all[j, src].reshape(2 * feats, tokens)
+                part += mm(left, cotan_all[src, j, :, cut], 1, 0)
+            if t == 3:
+                sums[:, :, cut] = part.reshape(2, feats, 256).astype(BF)
+            else:
+                total[:, cut] = part
+            return carry
+
+        lax.fori_loop(0, 8 * width // 256, tile, 0)
+
+    for t in range(7):
+        if t < 4:
+            first(t)
+        if 0 <= t - 1 < 4:
+            second(t - 1)
+        if 0 <= t - 2 < 4:
+            third(t - 2)
+        if 0 <= t - 3 < 4:
+            multiply(t - 3)
+
+    own = pltpu.make_async_copy(sums.at[:, :, mine], out_ref.at[:, x * 2 + c], own_sem.at[2])
+    own.start()
+    for i in (2, 1, 3, 0):
+        for flip in (0, 1):
+            if i or flip:
+                xx, cc = ring(x, i), lax.rem(c + flip, 2)
+                go(
+                    remote(
+                        sums.at[:, :, column(xx, cc)], out_ref.at[:, x * 2 + c],
+                        g_send.at[xx * 2 + cc], g_recv.at[x * 2 + c], x=xx, c=cc,
+                    )
+                )
+    for i in range(4):
+        for flip in range(2):
+            if i or flip:
+                at = ring(x, i) * 2 + lax.rem(c + flip, 2)
+                arrived(out_ref.at[:, at], g_recv.at[at])
+    own.wait()
+    for copy in started:
+        copy.wait_send()
+
+
+def gradient(acts, cotan, width):
+    feats, tokens = acts.shape
+    dma = pltpu.SemaphoreType.DMA
+    anywhere = pl.BlockSpec(memory_space=pl.ANY)
+    return pl.pallas_call(
+        gradient_kernel,
+        out_shape=jax.ShapeDtypeStruct((2, 8, feats, width), BF),
+        in_specs=[anywhere, anywhere],
+        out_specs=anywhere,
+        scratch_shapes=[
+            pltpu.VMEM((4, 4, 2, feats, tokens), BF),
+            pltpu.VMEM((4, 4, tokens, 8 * width), BF),
+            pltpu.VMEM((2 * feats, 8 * width), F32),
+            pltpu.VMEM((2, feats, 8 * width), BF),
+            dma((3,)),
+            dma((8,)), dma((8,)),
+            dma((3, 4)), dma((3, 4)),
+            dma((16,)), dma((16,)),
+            dma((3, 4)), dma((3, 4)),
+            dma((4, 4)), dma((4, 4)),
+            dma((8,)), dma((8,)),
+        ],
+        compiler_params=pltpu.CompilerParams(
+            collective_id=0, has_side_effects=True, vmem_limit_bytes=48 << 20
+        ),
+    )(acts, cotan)
+
+
 def per_device(acts, cotan, sketch_basis, sketch_values, start_basis):
-    gathered = lax.all_gather(acts, ("zl", "x", "c"), axis=1, tiled=True)
     shares = lax.axis_size("zh") * lax.axis_size("y")
-    grad = lax.psum_scatter(
-        lax.dot_general(
-            cotan, gathered, (((0,), (0,)), ((), ())), preferred_element_type=F32
-        ).astype(BF),
-        ("zh", "y"),
-        scatter_dimension=0,
-        tiled=True,
-    ).T
+    width = cotan.shape[1] // shares
+    grad = gradient(acts.T, cotan, width).reshape(-1, width)
     basis, values, update = sketch(grad, sketch_basis[0, 0], sketch_values[0], start_basis[0, 0])
     update = exchange(update, shares)
     return basis[None, None], values[None], update

time: 375 us -> 172 us (0.46)
  waiting for transfers between devices: 270 us -> 0 us
  Pallas kernels: 73 us -> 164 us
  between operations: 14.1 us -> 0.68 us
  matrix products: 10.8 us -> 0 us
    unnamed x3 -> x0, waiting for transfers between devices: 229 us -> none
    pallas_call x0 -> x1, Pallas kernels: none -> 94.3 us  [gradient(): pl.pallas_call(gradient_kernel, out_shape=jax.ShapeDtypeStruct((2, 8, fea...]
    all_gather x1 -> x0, waiting for transfers between devices: 41.3 us -> none  [per_device(): gathered = lax.all_gather(acts, ('zl', 'x', 'c'), axis=1, tiled=True)]
    dot_general x1 -> x0, matrix products: 10.8 us -> none  [per_device(): lax.dot_general(cotan, gathered, (((0,), (0,)), ((), ())), preferred_elem...]
  transfers between devices with their start and end apart: 2 -> 0, of which waited for: 2 -> 0; matrix products, arithmetic and copies ran while one was open for 0% -> 0% of each run, Pallas kernels for 0% -> 0%
where the time goes in v2:
time: 172 us; the launch traced here: 170 us
  Pallas kernels  164 us (95%)
  local copies, waits for them, and re-layouts  5.56 us (3%)
    pallas_call x1, Pallas kernels, gradient(): pl.pallas_call(gradient_kernel, out_shape=jax.ShapeDtypeStruct((2, 8, fea...  94.3 us
    pallas_call x1, Pallas kernels, sketch(): pl.pallas_call(sketch_kernel, out_shape=(jax.ShapeDtypeStruct((rank, dept...  35.1 us
    pallas_call x1, Pallas kernels, exchange(): pl.pallas_call(functools.partial(exchange_kernel, shares), out_shape=jax....  34.8 us
    unnamed x11, local copies, waits for them, and re-layouts  5.56 us

profile of v2, /device:TPU:26, one launch (start us, length us, event | category | flops | bytes accessed | tf_op | source)
XLA Modules:
  0.0 170.4 jit_solution(13426941766881140378)
XLA Ops:
  0.6 0.0 copy-start.2
  0.6 1.2 copy-done.2
  1.9 0.0 copy-start.3
  1.9 0.9 copy-done.3
  2.8 0.0 copy-start
  2.8 0.0 copy-start.4
  2.8 94.3 %shard_map.76 = bf16[2,8,288,128]{3,2,1,0:T(8,128)(2,1)S(1)} custom-call(bf16[288,256]{1,0:T(8,128)(2,1)S(1)} %bitcast.9, bf16[256,2048]{1,0:T(8,128)(2,1)S(1)} %copy-done.2), custom_call_target="tpu_custom_call" | custom-call | tf_op jit(solution)/shard_map/pallas_call | solution.py:407
  97.1 0.0 copy-done
  97.1 0.0 copy-done.4
  97.1 35.1 %shard_map.77 = (bf16[256,4608]{1,0:T(8,128)(2,1)}, f32[1,256]{1,0:T(1,128)}, bf16[4608,128]{1,0:T(8,128)(2,1)S(1)}) custom-call(bf16[4608,128]{1,0:T(8,128)(2,1)S(1)} %bitcast.7, bf16[256,4608]{1,0:T(8,128)(2,1)S(1)} %bitcast.8, f32[1,256]{1,0:T(1,128)S(1)} %bitcast.10, bf16[256,4608]{1,0:T(8,128)(2,1)} %bitcast.11), custom_call_target="tpu_custom_call" | custom-call | tf_op jit(solution)/shard_map/pallas_call | solution.py:157
  132.2 0.0 copy-start.1
  132.2 1.0 copy-done.1
  133.2 34.8 %shard_map.78 = bf16[288,2048]{1,0:T(8,128)(2,1)} custom-call(bf16[4608,128]{1,0:T(8,128)(2,1)} %copy-done.1), custom_call_target="tpu_custom_call" | custom-call | tf_op jit(solution)/shard_map/pallas_call | solution.py:213
  168.0 2.4 %copy.9 = bf16[288,2048]{1,0:T(8,128)(2,1)} copy(bf16[288,2048]{1,0:T(8,128)(2,1)} %shard_map.78) | data formatting | bytes 2359296
Async XLA Ops:
  0.6 1.2 copy-start.2
  1.9 0.9 copy-start.3
  2.8 94.4 %copy-start = (bf16[1,1,256,4608]{3,2,1,0:T(8,128)(2,1)S(1)}, bf16[1,1,256,4608]{3,2,1,0:T(8,128)(2,1)}, u32[]{:S(2)}) copy-start(bf16[1,1,256,4608]{3,2,1,0:T(8,128)(2,1)} %param.7) | copy-start | bytes 7077892
  2.8 94.4 %copy-start.4 = (f32[1,1,256]{2,1,0:T(1,128)S(1)}, f32[1,1,256]{2,1,0:T(1,128)}, u32[]{:S(2)}) copy-start(f32[1,1,256]{2,1,0:T(1,128)} %param.8) | copy-start | bytes 3076
  132.2 1.0 copy-start.1

commit v3 on v1

--- a/solution.py
+++ b/solution.py
@@ -10,6 +10,7 @@
 HIGH = lax.Precision.HIGHEST
 F32, BF = jnp.float32, jnp.bfloat16
 EPSILON = 1e-05
+VMEM_LIMIT = 60 << 20
 MESH = pl.DeviceIdType.MESH
 PANEL = 8
 
@@ -85,47 +86,20 @@
     return solve
 
 
-def sketch_kernel(grad_ref, basis_ref, values_ref, start_ref, new_ref, energy_ref, update_ref, scaled_ref):
-    rank, depth = basis_ref.shape
-    width = grad_ref.shape[1]
+def sketch_kernel(grad_ref, scaled_ref, gram_ref, coords_ref, new_ref, energy_ref, update_ref):
+    rank, depth = scaled_ref.shape
     step = 512
     eye = lax.broadcasted_iota(jnp.int32, (rank, rank), 0) == lax.broadcasted_iota(
         jnp.int32, (rank, rank), 1
     )
-    root = jnp.sqrt(jnp.sum(jnp.where(eye, values_ref[...], 0.0), axis=1, keepdims=True))
-
-    gram_bb = jnp.zeros((rank, rank), F32)
-    coord_b = jnp.zeros((rank, rank), F32)
-    gram_bg = jnp.zeros((rank, width), F32)
-    coord_g = jnp.zeros((rank, width), F32)
-    gram_gg = jnp.zeros((width, width), F32)
-    for at in range(0, depth, step):
-        cut = slice(at, at + step)
-        scaled = (root * basis_ref[:, cut].astype(F32)).astype(BF)
-        scaled_ref[:, cut] = scaled
-        start = start_ref[:, cut]
-        grad = grad_ref[cut, :]
-        gram_bb += mm(scaled, scaled, 1, 1)
-        coord_b += mm(start, scaled, 1, 1)
-        gram_bg += mm(scaled, grad, 1, 0)
-        coord_g += mm(start, grad, 1, 0)
-        gram_gg += mm(grad, grad, 0, 0)
-    gram = jnp.concatenate(
-        [
-            jnp.concatenate([gram_bb, gram_bg], axis=1),
-            jnp.concatenate([gram_bg.T, gram_gg], axis=1),
-        ],
-        axis=0,
-    )
-    gram_parts = split(gram)
+    gram_parts = split(gram_ref[...])
 
     def sweep(coords):
         mapped = sum(mm(coords, part, 1, 0) for part in gram_parts)
         images_gram = sum(mm(part, coords, 1, 1) for part in split(mapped))
         return mapped, solver(images_gram)
 
-    coords = jnp.concatenate([coord_b, coord_g], axis=1).astype(BF)
-    mapped, solve = sweep(coords)
+    mapped, solve = sweep(coords_ref[...])
     coords = solve(mapped).astype(BF)
     mapped, solve = sweep(coords)
     total = coords.shape[1]
@@ -150,8 +124,8 @@
         update_ref[cut, :] = (grad.astype(F32) + mm(basis, weights, 0, 0)).astype(BF)
 
 
-def sketch(grad, basis, values, start):
-    rank, depth = basis.shape
+def sketch(grad, scaled, gram, coords):
+    rank, depth = scaled.shape
     width = grad.shape[1]
     vmem = pl.BlockSpec(memory_space=pltpu.VMEM)
     return pl.pallas_call(
@@ -163,9 +137,8 @@
         ),
         in_specs=[vmem] * 4,
         out_specs=(vmem, vmem, vmem),
-        scratch_shapes=[pltpu.VMEM((rank, depth), BF)],
-        compiler_params=pltpu.CompilerParams(vmem_limit_bytes=48 << 20),
-    )(grad, basis, values, start)
+        compiler_params=pltpu.CompilerParams(vmem_limit_bytes=VMEM_LIMIT),
+    )(grad, scaled, gram, coords)
 
 
 def exchange_kernel(shares, update_ref, out_ref, own_sem, send_sem, recv_sem):
@@ -220,22 +193,350 @@
             pltpu.SemaphoreType.DMA((shares,)),
             pltpu.SemaphoreType.DMA((shares,)),
         ],
-        compiler_params=pltpu.CompilerParams(collective_id=1, has_side_effects=True),
+        compiler_params=pltpu.CompilerParams(
+            collective_id=1, has_side_effects=True, vmem_limit_bytes=VMEM_LIMIT
+        ),
     )(update)
 
 
+def gradient_kernel(
+    acts_ref, cotan_ref, basis_ref, values_ref, start_ref, grad_out, scaled_out, gram_ref, coords_ref,
+    acts_all, cotan_all, total, sums, grad_ref, basis_in, start_in, gram_bb, coord_b,
+    own_sem, z_send, z_recv, y_send, y_recv, d_send, d_recv, x_send, x_recv,
+    c_send, c_recv, g_send, g_recv,
+):
+    zh, y, zl, x, c = (lax.axis_index(name) for name in ("zh", "y", "zl", "x", "c"))
+    z = zh * 2 + zl
+    feats, tokens = acts_ref.shape
+    width = grad_ref.shape[-1]
+    rank, depth = basis_ref.shape
+
+    def ring(value, shift):
+        return lax.rem(value + shift, 4)
+
+    def line(shift):
+        at = lax.rem(z + shift + 8, 8)
+        return {"zh": at // 2, "zl": lax.rem(at, 2)}
+
+    def remote(src, dst, send, recv, where):
+        return pltpu.make_async_remote_copy(
+            src_ref=src, dst_ref=dst, send_sem=send, recv_sem=recv, device_id=where, device_id_type=MESH
+        )
+
+    load_basis = pltpu.make_async_copy(basis_ref, basis_in, own_sem.at[3])
+    load_start = pltpu.make_async_copy(start_ref, start_in, own_sem.at[4])
+    save_scaled = pltpu.make_async_copy(basis_in, scaled_out, own_sem.at[5])
+    save_grad = pltpu.make_async_copy(grad_ref, grad_out, own_sem.at[6])
+    load_basis.start()
+    load_start.start()
+
+    barrier = pltpu.get_barrier_semaphore()
+    greeted = 0
+    for i in range(4):
+        others = [{"zh": ring(zh, i), "y": ring(y, j)} for j in range(4) if i or j]
+        others += [{"x": ring(x, i), "c": lax.rem(c + j, 2)} for j in range(2) if i or j]
+        others += [{"zh": ring(zh, i), "zl": 1 - zl}]
+        for where in others:
+            pl.semaphore_signal(barrier, inc=1, device_id=where, device_id_type=MESH)
+        greeted += len(others)
+    pl.semaphore_wait(barrier, greeted)
+
+    started = []
+
+    def go(copy):
+        copy.start()
+        started.append(copy)
+
+    def arrived(dst, sem):
+        remote(dst, dst, sem, sem, {"x": ring(x, 1)}).wait_recv()
+
+    def column(xx, cc):
+        return pl.ds(pl.multiple_of((xx * 2 + cc) * width, width), width)
+
+    mine = column(x, c)
+    half = feats // 2
+
+    def acts_piece(yy, shift):
+        at = line(shift)
+        return acts_all.at[yy, at["zh"], at["zl"]]
+
+    def along_z(src, shift, hop):
+        ways = []
+        if shift <= 0:
+            ways.append((0, 1, slice(0, half) if hop == 4 else slice(0, feats)))
+        if shift >= 0:
+            ways.append((1, -1, slice(half, feats) if hop == 4 else slice(0, feats)))
+        for way, to, rows in ways:
+            go(
+                remote(
+                    src.at[rows], acts_piece(y, shift).at[rows],
+                    z_send.at[way, hop - 1], z_recv.at[way, hop - 1], line(to),
+                )
+            )
+
+    def along_y(src, dst, shift):
+        slot = shift + 3
+        go(remote(src, dst, y_send.at[0, slot], y_recv.at[0, slot], {"y": ring(y, 1)}))
+        go(remote(src, dst, y_send.at[1, slot], y_recv.at[1, slot], {"y": ring(y, 3)}))
+
+    def acts_first(hop):
+        if hop < 4:
+            for way, shift in ((0, -hop), (1, hop)):
+                piece = acts_piece(y, shift)
+                arrived(piece, z_recv.at[way, hop - 1])
+                along_z(piece, shift, hop + 1)
+                along_y(piece, piece, shift)
+        else:
+            piece = acts_piece(y, 4)
+            arrived(piece.at[slice(0, half)], z_recv.at[0, 3])
+            arrived(piece.at[slice(half, feats)], z_recv.at[1, 3])
+            along_y(piece, piece, 4)
+
+    def acts_second(shift):
+        slot = shift + 3
+        up = slot % 2
+        for k, back in enumerate((3, 1)):
+            piece = acts_piece(ring(y, back), shift)
+            arrived(piece, y_recv.at[k, slot])
+            if k == up:
+                go(remote(piece, piece, y_send.at[2, slot], y_recv.at[2, slot], {"y": ring(y, 4 - back)}))
+
+    def acts_third(shift):
+        arrived(acts_piece(ring(y, 2), shift), y_recv.at[2, shift + 3])
+
+    def cotan_piece(to_zh, to_y):
+        return cotan_ref.at[:, pl.ds(pl.multiple_of((to_zh * 4 + to_y) * width, width), width)]
+
+    def cotan_direct(r, js=(1, 3, 2, 0)):
+        for j in js:
+            if r or j:
+                to_zh, to_y = ring(zh, r), ring(y, j)
+                go(
+                    remote(
+                        cotan_piece(to_zh, to_y), cotan_all.at[zh, y, :, mine],
+                        d_send.at[r * 4 + j], d_recv.at[zh * 4 + y], {"zh": to_zh, "y": to_y},
+                    )
+                )
+
+    def cotan_first(r):
+        src = ring(zh, r)
+        for j in range(4):
+            if r or j:
+                yy = ring(y, j)
+                arrived(cotan_all.at[src, yy, :, mine], d_recv.at[src * 4 + yy])
+            else:
+                own_cotan.wait()
+        block = cotan_all.at[src, :, :, mine]
+        go(remote(block, block, x_send.at[0, r], x_recv.at[0, r], {"x": ring(x, 1)}))
+        go(remote(block, block, x_send.at[1, r], x_recv.at[1, r], {"x": ring(x, 3)}))
+        go(remote(block, block, c_send.at[0, r], c_recv.at[0, r], {"c": 1 - c}))
+
+    def cotan_second(r):
+        src = ring(zh, r)
+        up = r // 2
+        for k, back in enumerate((3, 1)):
+            block = cotan_all.at[src, :, :, column(ring(x, back), c)]
+            arrived(block, x_recv.at[k, r])
+            if k == up:
+                go(remote(block, block, x_send.at[2, r], x_recv.at[2, r], {"x": ring(x, 4 - back)}))
+            go(remote(block, block, c_send.at[back, r], c_recv.at[back, r], {"c": 1 - c}))
+
+    def cotan_third(r):
+        block = cotan_all.at[ring(zh, r), :, :, column(ring(x, 2), c)]
+        arrived(block, x_recv.at[2, r])
+        go(remote(block, block, c_send.at[2, r], c_recv.at[2, r], {"c": 1 - c}))
+
+    def multiply(r, begin, end):
+        src = ring(zh, r)
+        for shift in range(4):
+            arrived(cotan_all.at[src, :, :, column(ring(x, shift), 1 - c)], c_recv.at[shift, r])
+
+        def tile(n, carry):
+            cut = pl.ds(pl.multiple_of(n * 256, 256), 256)
+            part = jnp.zeros((2 * feats, 256), F32) if begin else total[:, cut]
+            for j in range(4):
+                left = acts_all[j, src].reshape(2 * feats, tokens)
+                part += mm(left, cotan_all[src, j, :, cut], 1, 0)
+            if end:
+                sums[:, :, cut] = part.reshape(2, feats, 256).astype(BF)
+            else:
+                total[:, cut] = part
+            return carry
+
+        if not end:
+            lax.fori_loop(0, 8 * width // 256, tile, 0)
+            return
+        for i in (2, 1, 3, 0):
+            xx = ring(x, i)
+            tile(xx, 0)
+            for flip in (0, 1):
+                if i or flip:
+                    cc = lax.rem(c + flip, 2)
+                    go(
+                        remote(
+                            sums.at[:, :, column(xx, cc)], grad_ref.at[:, x * 2 + c],
+                            g_send.at[xx * 2 + cc], g_recv.at[x * 2 + c], {"x": xx, "c": cc},
+                        )
+                    )
+
+    chunk, chunks = 512, depth // 512
+
+    def prepare(begin, end):
+        if begin == 0:
+            load_basis.wait()
+            load_start.wait()
+            gram_bb[...] = jnp.zeros_like(gram_bb)
+            coord_b[...] = jnp.zeros_like(coord_b)
+        eye = lax.broadcasted_iota(jnp.int32, (rank, rank), 0) == lax.broadcasted_iota(
+            jnp.int32, (rank, rank), 1
+        )
+        root = jnp.sqrt(jnp.sum(jnp.where(eye, values_ref[...], 0.0), axis=1, keepdims=True))
+
+        def one(n, carry):
+            cut = pl.ds(pl.multiple_of(n * chunk, chunk), chunk)
+            scaled = (root * basis_in[:, cut].astype(F32)).astype(BF)
+            basis_in[:, cut] = scaled
+            gram_bb[...] += mm(scaled, scaled, 1, 1)
+            coord_b[...] += mm(start_in[:, cut], scaled, 1, 1)
+            return carry
+
+        lax.fori_loop(begin, end, one, 0)
+        if end == chunks:
+            save_scaled.start()
+
+    own_piece = acts_piece(y, 0)
+    own_acts = pltpu.make_async_copy(acts_ref, own_piece, own_sem.at[0])
+    own_cotan = pltpu.make_async_copy(cotan_piece(zh, y), cotan_all.at[zh, y, :, mine], own_sem.at[1])
+
+    along_z(acts_ref, 0, 1)
+    along_y(acts_ref, own_piece, 0)
+    cotan_direct(0)
+    own_acts.start()
+    own_cotan.start()
+    own_acts.wait()
+    prepare(0, 3)
+    acts_first(1)
+    cotan_direct(1)
+    cotan_direct(3)
+    cotan_first(0)
+    prepare(3, 6)
+    acts_second(0)
+    acts_first(2)
+    cotan_second(0)
+    prepare(6, 9)
+    acts_second(1)
+    acts_second(-1)
+    cotan_direct(2, (1, 3))
+    cotan_first(1)
+    cotan_first(3)
+    acts_first(3)
+    cotan_direct(2, (2, 0))
+    acts_second(2)
+    acts_second(-2)
+    cotan_third(0)
+    cotan_second(1)
+    cotan_second(3)
+    acts_first(4)
+    cotan_first(2)
+    acts_second(3)
+    acts_second(-3)
+    acts_third(0)
+    acts_third(1)
+    acts_third(-1)
+    multiply(0, True, False)
+    acts_second(4)
+    cotan_third(1)
+    cotan_third(3)
+    cotan_second(2)
+    acts_third(2)
+    acts_third(-2)
+    acts_third(3)
+    acts_third(-3)
+    multiply(1, False, False)
+    cotan_third(2)
+    multiply(3, False, False)
+    acts_third(4)
+    multiply(2, False, True)
+
+    own = pltpu.make_async_copy(sums.at[:, :, mine], grad_ref.at[:, x * 2 + c], own_sem.at[2])
+    own.start()
+    own.wait()
+    for i in (0, 1, 3, 2):
+        for flip in range(2):
+            if i or flip:
+                at = ring(x, i) * 2 + lax.rem(c + flip, 2)
+                arrived(grad_ref.at[:, at], g_recv.at[at])
+    save_grad.start()
+
+    gram_bg = jnp.zeros((rank, width), F32)
+    coord_g = jnp.zeros((rank, width), F32)
+    gram_gg = jnp.zeros((width, width), F32)
+    grad = grad_ref[...].reshape(depth, width)
+    for at in range(0, depth, chunk):
+        cut = slice(at, at + chunk)
+        part = grad[cut]
+        gram_bg += mm(basis_in[:, cut], part, 1, 0)
+        coord_g += mm(start_in[:, cut], part, 1, 0)
+        gram_gg += mm(part, part, 0, 0)
+    gram_ref[:rank, :rank] = gram_bb[...]
+    gram_ref[:rank, rank:] = gram_bg
+    gram_ref[rank:, :rank] = gram_bg.T
+    gram_ref[rank:, rank:] = gram_gg
+    coords_ref[:, :rank] = coord_b[...].astype(BF)
+    coords_ref[:, rank:] = coord_g.astype(BF)
+    save_scaled.wait()
+    save_grad.wait()
+    for copy in started:
+        copy.wait_send()
+
+
+def gradient(acts, cotan, basis, values, start, width):
+    feats, tokens = acts.shape
+    rank, depth = basis.shape
+    dma = pltpu.SemaphoreType.DMA
+    anywhere = pl.BlockSpec(memory_space=pl.ANY)
+    vmem = pl.BlockSpec(memory_space=pltpu.VMEM)
+    return pl.pallas_call(
+        gradient_kernel,
+        out_shape=(
+            jax.ShapeDtypeStruct((2, 8, feats, width), BF),
+            jax.ShapeDtypeStruct((rank, depth), BF),
+            jax.ShapeDtypeStruct((rank + width, rank + width), F32),
+            jax.ShapeDtypeStruct((rank, rank + width), BF),
+        ),
+        in_specs=[anywhere, anywhere, anywhere, vmem, anywhere],
+        out_specs=(anywhere, anywhere, vmem, vmem),
+        scratch_shapes=[
+            pltpu.VMEM((4, 4, 2, feats, tokens), BF),
+            pltpu.VMEM((4, 4, tokens, 8 * width), BF),
+            pltpu.VMEM((2 * feats, 8 * width), F32),
+            pltpu.VMEM((2, feats, 8 * width), BF),
+            pltpu.VMEM((2, 8, feats, width), BF),
+            pltpu.VMEM((rank, depth), BF),
+            pltpu.VMEM((rank, depth), BF),
+            pltpu.VMEM((rank, rank), F32),
+            pltpu.VMEM((rank, rank), F32),
+            dma((7,)),
+            dma((2, 4)), dma((2, 4)),
+            dma((3, 8)), dma((3, 8)),
+            dma((16,)), dma((16,)),
+            dma((3, 4)), dma((3, 4)),
+            dma((4, 4)), dma((4, 4)),
+            dma((8,)), dma((8,)),
+        ],
+        compiler_params=pltpu.CompilerParams(
+            collective_id=0, has_side_effects=True, vmem_limit_bytes=VMEM_LIMIT
+        ),
+    )(acts, cotan, basis, values, start)
+
+
 def per_device(acts, cotan, sketch_basis, sketch_values, start_basis):
-    gathered = lax.all_gather(acts, ("zl", "x", "c"), axis=1, tiled=True)
     shares = lax.axis_size("zh") * lax.axis_size("y")
-    grad = lax.psum_scatter(
-        lax.dot_general(
-            cotan, gathered, (((0,), (0,)), ((), ())), preferred_element_type=F32
-        ).astype(BF),
-        ("zh", "y"),
-        scatter_dimension=0,
-        tiled=True,
-    ).T
-    basis, values, update = sketch(grad, sketch_basis[0, 0], sketch_values[0], start_basis[0, 0])
+    width = cotan.shape[1] // shares
+    grad, scaled, gram, coords = gradient(
+        acts.T, cotan, sketch_basis[0, 0], sketch_values[0], start_basis[0, 0], width
+    )
+    basis, values, update = sketch(grad.reshape(-1, width), scaled, gram, coords)
     update = exchange(update, shares)
     return basis[None, None], values[None], update
 

time: 375 us -> 155 us (0.41)
  waiting for transfers between devices: 270 us -> 0 us
  Pallas kernels: 73 us -> 152 us
  between operations: 14.1 us -> 0.65 us
  matrix products: 10.8 us -> 0 us
  local copies, waits for them, and re-layouts: 7.04 us -> 2.41 us
    unnamed x3 -> x0, waiting for transfers between devices: 229 us -> none
    pallas_call x0 -> x1, Pallas kernels: none -> 85.6 us  [gradient(): pl.pallas_call(gradient_kernel, out_shape=(jax.ShapeDtypeStruct((2, 8, fe...]
    all_gather x1 -> x0, waiting for transfers between devices: 41.3 us -> none  [per_device(): gathered = lax.all_gather(acts, ('zl', 'x', 'c'), axis=1, tiled=True)]
    dot_general x1 -> x0, matrix products: 10.8 us -> none  [per_device(): lax.dot_general(cotan, gathered, (((0,), (0,)), ((), ())), preferred_elem...]
    unnamed x10 -> x1, local copies, waits for them, and re-layouts: 7.04 us -> 2.41 us
  transfers between devices with their start and end apart: 2 -> 0, of which waited for: 2 -> 0; matrix products, arithmetic and copies ran while one was open for 0% -> 0% of each run, Pallas kernels for 0% -> 0%
where the time goes in v3:
time: 155 us
  Pallas kernels  152 us (98%)
  local copies, waits for them, and re-layouts  2.41 us (2%)
    pallas_call x1, Pallas kernels, gradient(): pl.pallas_call(gradient_kernel, out_shape=(jax.ShapeDtypeStruct((2, 8, fe...  85.6 us
    pallas_call x1, Pallas kernels, exchange(): pl.pallas_call(functools.partial(exchange_kernel, shares), out_shape=jax....  34.9 us
    pallas_call x1, Pallas kernels, sketch(): pl.pallas_call(sketch_kernel, out_shape=(jax.ShapeDtypeStruct((rank, dept...  31.7 us

profile of v3, /device:TPU:26, one launch (start us, length us, event | category | flops | bytes accessed | tf_op | source)
XLA Modules:
  0.0 155.3 jit_solution(9167865393420737833)
XLA Ops:
  0.6 85.6 %shard_map.76 = (bf16[2,8,288,128]{3,2,1,0:T(8,128)(2,1)}, bf16[256,4608]{1,0:T(8,128)(2,1)}, f32[384,384]{1,0:T(8,128)}, bf16[256,384]{1,0:T(8,128)(2,1)}) custom-call(bf16[288,256]{1,0:T(8,128)(2,1)} %bitcast.10, bf16[256,2048]{1,0:T(8,128)(2,1)} %cotan_ref.1, bf16[256,4608]{1,0:T(8,128)(2,1)} %bitcast.7, f32[1,256]{1,0:T(1,128)} %bitcast.11, ...), custom_call_target="tpu_custom_call" | custom-call | tf_op jit(solution)/shard_map/pallas_call | solution.py:499
  86.3 31.7 %shard_map.77 = (bf16[256,4608]{1,0:T(8,128)(2,1)}, f32[1,256]{1,0:T(1,128)}, bf16[4608,128]{1,0:T(8,128)(2,1)}) custom-call(bf16[4608,128]{1,0:T(8,128)(2,1)} %bitcast.9, bf16[256,4608]{1,0:T(8,128)(2,1)} %get-tuple-element.11.scaled_ref, f32[384,384]{1,0:T(8,128)} %get-tuple-element.12.gram_ref, bf16[256,384]{1,0:T(8,128)(2,1)} %get-tuple-element.13.coords_ref), custom_call_target="tpu_custom_call" | custom-call | tf_op jit(solution)/shard_map/pallas_call | solution.py:131
  118.0 34.9 %shard_map.78 = bf16[288,2048]{1,0:T(8,128)(2,1)} custom-call(bf16[4608,128]{1,0:T(8,128)(2,1)} %get-tuple-element.16.update_ref), custom_call_target="tpu_custom_call" | custom-call | tf_op jit(solution)/shard_map/pallas_call | solution.py:186
  152.9 2.4 %copy.9 = bf16[288,2048]{1,0:T(8,128)(2,1)} copy(bf16[288,2048]{1,0:T(8,128)(2,1)} %shard_map.78) | data formatting | bytes 2359296

commit v4 on v3

--- a/solution.py
+++ b/solution.py
@@ -86,57 +86,84 @@
     return solve
 
 
-def sketch_kernel(grad_ref, scaled_ref, gram_ref, coords_ref, new_ref, energy_ref, update_ref):
-    rank, depth = scaled_ref.shape
-    step = 512
+def sketch_kernel(
+    grad_ref, scaled_ref, gram_ref, coords_ref, new_ref, energy_ref, update_ref, combine_ref, weights_ref
+):
+    rank = gram_ref.shape[0] - grad_ref.shape[1]
+
+    @pl.when(pl.program_id(0) == 0)
+    def _():
+        combine, weights, energy_ref[...] = sketch_step(gram_ref[...], coords_ref[...], rank)
+        for n, part in enumerate(combine):
+            combine_ref[n] = part
+        weights_ref[...] = weights
+
+    step = 384
+    for at in range(0, scaled_ref.shape[1], step):
+        cut = slice(at, at + step)
+        grad = grad_ref[cut, :]
+        scaled = scaled_ref[:, cut]
+        basis = sum(mm(combine_ref[n, :, :rank], scaled, 1, 0) for n in range(2))
+        basis += sum(mm(combine_ref[n, :, rank:], grad, 1, 1) for n in range(2))
+        basis = basis.astype(BF)
+        new_ref[:, cut] = basis
+        update_ref[cut, :] = (grad.astype(F32) + mm(basis, weights_ref[...], 0, 0)).astype(BF)
+
+
+def sketch_step(gram, coords, rank):
     eye = lax.broadcasted_iota(jnp.int32, (rank, rank), 0) == lax.broadcasted_iota(
         jnp.int32, (rank, rank), 1
     )
-    gram_parts = split(gram_ref[...])
+    gram_parts = split(gram)
 
     def sweep(coords):
         mapped = sum(mm(coords, part, 1, 0) for part in gram_parts)
         images_gram = sum(mm(part, coords, 1, 1) for part in split(mapped))
         return mapped, solver(images_gram)
 
-    mapped, solve = sweep(coords_ref[...])
+    mapped, solve = sweep(coords)
     coords = solve(mapped).astype(BF)
     mapped, solve = sweep(coords)
     total = coords.shape[1]
     solved = solve(jnp.concatenate([coords.astype(F32), mapped], axis=1))
-    combine = split(solved[:, :total])
+    combine = split(solved[:, :total], 2)
     final = solved[:, total:]
     square = final * final
     energy = jnp.sum(square, axis=1, keepdims=True)
     lowest = jnp.min(energy)
     energy_row = jnp.sum(jnp.where(eye, energy, 0.0), axis=0, keepdims=True)
-    energy_ref[...] = energy_row - lowest
     shrink = jnp.sqrt(jnp.sqrt((lowest + EPSILON) / energy)) - 1.0
     weights = (shrink * final[:, rank:]).astype(BF)
-    for at in range(0, depth, step):
-        cut = slice(at, at + step)
-        grad = grad_ref[cut, :]
-        scaled = scaled_ref[:, cut]
-        basis = sum(mm(part[:, :rank], scaled, 1, 0) for part in combine)
-        basis += sum(mm(part[:, rank:], grad, 1, 1) for part in combine)
-        basis = basis.astype(BF)
-        new_ref[:, cut] = basis
-        update_ref[cut, :] = (grad.astype(F32) + mm(basis, weights, 0, 0)).astype(BF)
+    return combine, weights, energy_row - lowest
 
 
 def sketch(grad, scaled, gram, coords):
     rank, depth = scaled.shape
     width = grad.shape[1]
-    vmem = pl.BlockSpec(memory_space=pltpu.VMEM)
+    block = depth // 3
     return pl.pallas_call(
         sketch_kernel,
+        grid=(depth // block,),
         out_shape=(
             jax.ShapeDtypeStruct((rank, depth), BF),
             jax.ShapeDtypeStruct((1, rank), F32),
             jax.ShapeDtypeStruct((depth, width), BF),
         ),
-        in_specs=[vmem] * 4,
-        out_specs=(vmem, vmem, vmem),
+        in_specs=[
+            pl.BlockSpec((block, width), lambda i: (i, 0)),
+            pl.BlockSpec((rank, block), lambda i: (0, i)),
+            pl.BlockSpec(gram.shape, lambda i: (0, 0)),
+            pl.BlockSpec(coords.shape, lambda i: (0, 0)),
+        ],
+        out_specs=(
+            pl.BlockSpec((rank, block), lambda i: (0, i)),
+            pl.BlockSpec((1, rank), lambda i: (0, 0)),
+            pl.BlockSpec((block, width), lambda i: (i, 0)),
+        ),
+        scratch_shapes=[
+            pltpu.VMEM((2, rank, rank + width), BF),
+            pltpu.VMEM((rank, width), BF),
+        ],
         compiler_params=pltpu.CompilerParams(vmem_limit_bytes=VMEM_LIMIT),
     )(grad, scaled, gram, coords)
 
@@ -254,7 +281,7 @@
         return pl.ds(pl.multiple_of((xx * 2 + cc) * width, width), width)
 
     mine = column(x, c)
-    half = feats // 2
+    parts = (slice(0, 160), slice(160, feats))
 
     def acts_piece(yy, shift):
         at = line(shift)
@@ -263,9 +290,9 @@
     def along_z(src, shift, hop):
         ways = []
         if shift <= 0:
-            ways.append((0, 1, slice(0, half) if hop == 4 else slice(0, feats)))
+            ways.append((0, 1, parts[0] if hop == 4 else slice(0, feats)))
         if shift >= 0:
-            ways.append((1, -1, slice(half, feats) if hop == 4 else slice(0, feats)))
+            ways.append((1, -1, parts[1] if hop == 4 else slice(0, feats)))
         for way, to, rows in ways:
             go(
                 remote(
@@ -274,10 +301,15 @@
                 )
             )
 
-    def along_y(src, dst, shift):
-        slot = shift + 3
-        go(remote(src, dst, y_send.at[0, slot], y_recv.at[0, slot], {"y": ring(y, 1)}))
-        go(remote(src, dst, y_send.at[1, slot], y_recv.at[1, slot], {"y": ring(y, 3)}))
+    def along_y(part, shift, src=None):
+        dst = acts_piece(y, shift).at[parts[part]]
+        src = dst if src is None else src.at[parts[part]]
+        for k, to in enumerate((1, 3)):
+            go(
+                remote(
+                    src, dst, y_send.at[k, part, shift + 3], y_recv.at[k, part, shift + 3], {"y": ring(y, to)}
+                )
+            )
 
     def acts_first(hop):
         if hop < 4:
@@ -285,24 +317,29 @@
                 piece = acts_piece(y, shift)
                 arrived(piece, z_recv.at[way, hop - 1])
                 along_z(piece, shift, hop + 1)
-                along_y(piece, piece, shift)
+                along_y(0, shift)
         else:
             piece = acts_piece(y, 4)
-            arrived(piece.at[slice(0, half)], z_recv.at[0, 3])
-            arrived(piece.at[slice(half, feats)], z_recv.at[1, 3])
-            along_y(piece, piece, 4)
-
-    def acts_second(shift):
+            for way in range(2):
+                arrived(piece.at[parts[way]], z_recv.at[way, 3])
+                along_y(way, 4)
+
+    def acts_second(part, shift):
         slot = shift + 3
         up = slot % 2
         for k, back in enumerate((3, 1)):
-            piece = acts_piece(ring(y, back), shift)
-            arrived(piece, y_recv.at[k, slot])
+            piece = acts_piece(ring(y, back), shift).at[parts[part]]
+            arrived(piece, y_recv.at[k, part, slot])
             if k == up:
-                go(remote(piece, piece, y_send.at[2, slot], y_recv.at[2, slot], {"y": ring(y, 4 - back)}))
-
-    def acts_third(shift):
-        arrived(acts_piece(ring(y, 2), shift), y_recv.at[2, shift + 3])
+                go(
+                    remote(
+                        piece, piece, y_send.at[2, part, slot], y_recv.at[2, part, slot],
+                        {"y": ring(y, 4 - back)},
+                    )
+                )
+
+    def acts_third(part, shift):
+        arrived(acts_piece(ring(y, 2), shift).at[parts[part]], y_recv.at[2, part, shift + 3])
 
     def cotan_piece(to_zh, to_y):
         return cotan_ref.at[:, pl.ds(pl.multiple_of((to_zh * 4 + to_y) * width, width), width)]
@@ -313,54 +350,63 @@
                 to_zh, to_y = ring(zh, r), ring(y, j)
                 go(
                     remote(
-                        cotan_piece(to_zh, to_y), cotan_all.at[zh, y, :, mine],
+                        cotan_piece(to_zh, to_y), cotan_all.at[zh, lax.rem(y, 2), y // 2, :, mine],
                         d_send.at[r * 4 + j], d_recv.at[zh * 4 + y], {"zh": to_zh, "y": to_y},
                     )
                 )
 
-    def cotan_first(r):
-        src = ring(zh, r)
-        for j in range(4):
+    def cotan_block(r, e, xx, cc):
+        return cotan_all.at[ring(zh, r), lax.rem(y + 1 + e, 2), :, :, column(xx, cc)]
+
+    def cotan_first(r, e):
+        for j in ((1, 3), (2, 0))[e]:
             if r or j:
-                yy = ring(y, j)
-                arrived(cotan_all.at[src, yy, :, mine], d_recv.at[src * 4 + yy])
+                src, yy = ring(zh, r), ring(y, j)
+                arrived(cotan_all.at[src, lax.rem(yy, 2), yy // 2, :, mine], d_recv.at[src * 4 + yy])
             else:
                 own_cotan.wait()
-        block = cotan_all.at[src, :, :, mine]
-        go(remote(block, block, x_send.at[0, r], x_recv.at[0, r], {"x": ring(x, 1)}))
-        go(remote(block, block, x_send.at[1, r], x_recv.at[1, r], {"x": ring(x, 3)}))
-        go(remote(block, block, c_send.at[0, r], c_recv.at[0, r], {"c": 1 - c}))
-
-    def cotan_second(r):
+        n = 2 * r + e
+        block = cotan_block(r, e, x, c)
+        go(remote(block, block, x_send.at[0, n], x_recv.at[0, n], {"x": ring(x, 1)}))
+        go(remote(block, block, x_send.at[1, n], x_recv.at[1, n], {"x": ring(x, 3)}))
+        go(remote(block, block, c_send.at[0, n], c_recv.at[0, n], {"c": 1 - c}))
+
+    def cotan_second(r, e):
+        n = 2 * r + e
+        for k, back in enumerate((3, 1)):
+            block = cotan_block(r, e, ring(x, back), c)
+            arrived(block, x_recv.at[k, n])
+            if k == e:
+                go(remote(block, block, x_send.at[2, n], x_recv.at[2, n], {"x": ring(x, 4 - back)}))
+            go(remote(block, block, c_send.at[back, n], c_recv.at[back, n], {"c": 1 - c}))
+
+    def cotan_third(r, e):
+        n = 2 * r + e
+        block = cotan_block(r, e, ring(x, 2), c)
+        arrived(block, x_recv.at[2, n])
+        go(remote(block, block, c_send.at[2, n], c_recv.at[2, n], {"c": 1 - c}))
+
+    def cotan_last(r):
+        for e in range(2):
+            for shift in range(4):
+                arrived(cotan_block(r, e, ring(x, shift), 1 - c), c_recv.at[shift, 2 * r + e])
+
+    def multiply(r, part, begin, end):
         src = ring(zh, r)
-        up = r // 2
-        for k, back in enumerate((3, 1)):
-            block = cotan_all.at[src, :, :, column(ring(x, back), c)]
-            arrived(block, x_recv.at[k, r])
-            if k == up:
-                go(remote(block, block, x_send.at[2, r], x_recv.at[2, r], {"x": ring(x, 4 - back)}))
-            go(remote(block, block, c_send.at[back, r], c_recv.at[back, r], {"c": 1 - c}))
-
-    def cotan_third(r):
-        block = cotan_all.at[ring(zh, r), :, :, column(ring(x, 2), c)]
-        arrived(block, x_recv.at[2, r])
-        go(remote(block, block, c_send.at[2, r], c_recv.at[2, r], {"c": 1 - c}))
-
-    def multiply(r, begin, end):
-        src = ring(zh, r)
-        for shift in range(4):
-            arrived(cotan_all.at[src, :, :, column(ring(x, shift), 1 - c)], c_recv.at[shift, r])
+        rows = parts[part]
+        count = rows.stop - rows.start
 
         def tile(n, carry):
             cut = pl.ds(pl.multiple_of(n * 256, 256), 256)
-            part = jnp.zeros((2 * feats, 256), F32) if begin else total[:, cut]
+            out = jnp.zeros((2 * count, 256), F32) if begin else total[:, rows, cut].reshape(2 * count, 256)
             for j in range(4):
-                left = acts_all[j, src].reshape(2 * feats, tokens)
-                part += mm(left, cotan_all[src, j, :, cut], 1, 0)
+                left = acts_all[j, src, :, rows].reshape(2 * count, tokens)
+                out += mm(left, cotan_all[src, j % 2, j // 2, :, cut], 1, 0)
+            out = out.reshape(2, count, 256)
             if end:
-                sums[:, :, cut] = part.reshape(2, feats, 256).astype(BF)
+                sums[:, rows, cut] = out.astype(BF)
             else:
-                total[:, cut] = part
+                total[:, rows, cut] = out
             return carry
 
         if not end:
@@ -374,8 +420,8 @@
                     cc = lax.rem(c + flip, 2)
                     go(
                         remote(
-                            sums.at[:, :, column(xx, cc)], grad_ref.at[:, x * 2 + c],
-                            g_send.at[xx * 2 + cc], g_recv.at[x * 2 + c], {"x": xx, "c": cc},
+                            sums.at[:, rows, column(xx, cc)], grad_ref.at[:, x * 2 + c, rows],
+                            g_send.at[part, xx * 2 + cc], g_recv.at[part, x * 2 + c], {"x": xx, "c": cc},
                         )
                     )
 
@@ -406,66 +452,109 @@
 
     own_piece = acts_piece(y, 0)
     own_acts = pltpu.make_async_copy(acts_ref, own_piece, own_sem.at[0])
-    own_cotan = pltpu.make_async_copy(cotan_piece(zh, y), cotan_all.at[zh, y, :, mine], own_sem.at[1])
+    own_cotan = pltpu.make_async_copy(cotan_piece(zh, y), cotan_all.at[zh, lax.rem(y, 2), y // 2, :, mine], own_sem.at[1])
 
     along_z(acts_ref, 0, 1)
-    along_y(acts_ref, own_piece, 0)
+    along_y(0, 0, acts_ref)
+    along_y(1, 0, acts_ref)
     cotan_direct(0)
     own_acts.start()
     own_cotan.start()
     own_acts.wait()
     prepare(0, 3)
+    prepare(3, 6)
     acts_first(1)
     cotan_direct(1)
     cotan_direct(3)
-    cotan_first(0)
-    prepare(3, 6)
-    acts_second(0)
+    cotan_first(0, 0)
+    cotan_first(0, 1)
+    along_y(1, 1)
+    along_y(1, -1)
+    acts_second(0, 0)
+    acts_second(1, 0)
     acts_first(2)
-    cotan_second(0)
+    cotan_second(0, 0)
+    cotan_second(0, 1)
+    acts_second(0, 1)
+    acts_second(0, -1)
     prepare(6, 9)
-    acts_second(1)
-    acts_second(-1)
-    cotan_direct(2, (1, 3))
-    cotan_first(1)
-    cotan_first(3)
+    cotan_direct(2)
+    cotan_first(1, 0)
+    cotan_first(3, 0)
+    cotan_first(1, 1)
+    cotan_first(3, 1)
     acts_first(3)
-    cotan_direct(2, (2, 0))
-    acts_second(2)
-    acts_second(-2)
-    cotan_third(0)
-    cotan_second(1)
-    cotan_second(3)
+    acts_second(0, 2)
+    acts_second(0, -2)
+    cotan_third(0, 0)
+    cotan_third(0, 1)
+    acts_second(1, 1)
+    acts_second(1, -1)
+    cotan_second(1, 0)
+    cotan_second(3, 0)
+    cotan_second(1, 1)
+    cotan_second(3, 1)
+    along_y(1, 2)
+    along_y(1, -2)
     acts_first(4)
-    cotan_first(2)
-    acts_second(3)
-    acts_second(-3)
-    acts_third(0)
-    acts_third(1)
-    acts_third(-1)
-    multiply(0, True, False)
-    acts_second(4)
-    cotan_third(1)
-    cotan_third(3)
-    cotan_second(2)
-    acts_third(2)
-    acts_third(-2)
-    acts_third(3)
-    acts_third(-3)
-    multiply(1, False, False)
-    cotan_third(2)
-    multiply(3, False, False)
-    acts_third(4)
-    multiply(2, False, True)
+    cotan_first(2, 0)
+    acts_third(0, 0)
+    acts_third(0, 1)
+    acts_third(0, -1)
+    cotan_last(0)
+    multiply(0, 0, True, False)
+    acts_second(0, 3)
+    acts_second(0, -3)
+    cotan_third(1, 0)
+    cotan_third(3, 0)
+    along_y(1, 3)
+    along_y(1, -3)
+    cotan_third(1, 1)
+    cotan_third(3, 1)
+    cotan_first(2, 1)
+    cotan_second(2, 0)
+    acts_second(0, 4)
+    acts_second(1, 2)
+    acts_second(1, -2)
+    acts_third(1, 0)
+    acts_third(1, 1)
+    acts_third(1, -1)
+    multiply(0, 1, True, False)
+    cotan_second(2, 1)
+    acts_third(0, 2)
+    acts_third(0, -2)
+    acts_third(0, 3)
+    acts_third(0, -3)
+    cotan_last(1)
+    multiply(1, 0, False, False)
+    cotan_last(3)
+    multiply(3, 0, False, False)
+    cotan_third(2, 0)
+    acts_second(1, 3)
+    acts_second(1, -3)
+    acts_third(0, 4)
+    cotan_third(2, 1)
+    cotan_last(2)
+    multiply(2, 0, False, True)
+    acts_second(1, 4)
+    acts_third(1, 2)
+    acts_third(1, -2)
+    acts_third(1, 3)
+    acts_third(1, -3)
+    multiply(1, 1, False, False)
+    multiply(3, 1, False, False)
+    acts_third(1, 4)
+    multiply(2, 1, False, True)
 
     own = pltpu.make_async_copy(sums.at[:, :, mine], grad_ref.at[:, x * 2 + c], own_sem.at[2])
     own.start()
     own.wait()
-    for i in (0, 1, 3, 2):
-        for flip in range(2):
-            if i or flip:
-                at = ring(x, i) * 2 + lax.rem(c + flip, 2)
-                arrived(grad_ref.at[:, at], g_recv.at[at])
+    for part in range(2):
+        for i in (0, 1, 3, 2):
+            for flip in range(2):
+                if i or flip:
+                    at = ring(x, i) * 2 + lax.rem(c + flip, 2)
+                    arrived(grad_ref.at[:, at, parts[part]], g_recv.at[part, at])
     save_grad.start()
 
     gram_bg = jnp.zeros((rank, width), F32)
@@ -508,8 +597,8 @@
         out_specs=(anywhere, anywhere, vmem, vmem),
         scratch_shapes=[
             pltpu.VMEM((4, 4, 2, feats, tokens), BF),
-            pltpu.VMEM((4, 4, tokens, 8 * width), BF),
-            pltpu.VMEM((2 * feats, 8 * width), F32),
+            pltpu.VMEM((4, 2, 2, tokens, 8 * width), BF),
+            pltpu.VMEM((2, feats, 8 * width), F32),
             pltpu.VMEM((2, feats, 8 * width), BF),
             pltpu.VMEM((2, 8, feats, width), BF),
             pltpu.VMEM((rank, depth), BF),
@@ -518,11 +607,11 @@
             pltpu.VMEM((rank, rank), F32),
             dma((7,)),
             dma((2, 4)), dma((2, 4)),
+            dma((3, 2, 8)), dma((3, 2, 8)),
+            dma((16,)), dma((16,)),
             dma((3, 8)), dma((3, 8)),
-            dma((16,)), dma((16,)),
-            dma((3, 4)), dma((3, 4)),
-            dma((4, 4)), dma((4, 4)),
-            dma((8,)), dma((8,)),
+            dma((4, 8)), dma((4, 8)),
+            dma((2, 8)), dma((2, 8)),
         ],
         compiler_params=pltpu.CompilerParams(
             collective_id=0, has_side_effects=True, vmem_limit_bytes=VMEM_LIMIT

time: 155 us -> 153 us (0.987)
  Pallas kernels: 152 us -> 149 us
    pallas_call x1, Pallas kernels: 85.6 us -> 81.1 us  [gradient(): pl.pallas_call(gradient_kernel, out_shape=(jax.ShapeDtypeStruct((2, 8, fe...]
    pallas_call x1, Pallas kernels: 34.9 us -> 39.2 us  [exchange(): pl.pallas_call(functools.partial(exchange_kernel, shares), out_shape=jax....]
    pallas_call x1, Pallas kernels: 31.7 us -> 28.5 us  [sketch(): pl.pallas_call(sketch_kernel, grid=(depth // block,), out_shape=(jax.Shap...]
where the time goes in v4:
time: 153 us; the launch traced here: 152 us
  Pallas kernels  149 us (97%)
  local copies, waits for them, and re-layouts  2.41 us (2%)
    pallas_call x1, Pallas kernels, gradient(): pl.pallas_call(gradient_kernel, out_shape=(jax.ShapeDtypeStruct((2, 8, fe...  81.1 us
    pallas_call x1, Pallas kernels, exchange(): pl.pallas_call(functools.partial(exchange_kernel, shares), out_shape=jax....  39.2 us
    pallas_call x1, Pallas kernels, sketch(): pl.pallas_call(sketch_kernel, grid=(depth // block,), out_shape=(jax.Shap...  28.5 us

profile of v4, /device:TPU:26, one launch (start us, length us, event | category | flops | bytes accessed | tf_op | source)
XLA Modules:
  0.0 151.9 jit_solution(2137209703838084794)
XLA Ops:
  0.6 81.1 %shard_map.76 = (bf16[2,8,288,128]{3,2,1,0:T(8,128)(2,1)}, bf16[256,4608]{1,0:T(8,128)(2,1)}, f32[384,384]{1,0:T(8,128)}, bf16[256,384]{1,0:T(8,128)(2,1)}) custom-call(bf16[288,256]{1,0:T(8,128)(2,1)} %bitcast.10, bf16[256,2048]{1,0:T(8,128)(2,1)} %cotan_ref.1, bf16[256,4608]{1,0:T(8,128)(2,1)} %bitcast.7, f32[1,256]{1,0:T(1,128)} %bitcast.11, ...), custom_call_target="tpu_custom_call" | custom-call | tf_op jit(solution)/shard_map/pallas_call | solution.py:588
  81.7 28.5 %shard_map.77 = (bf16[256,4608]{1,0:T(8,128)(2,1)}, f32[1,256]{1,0:T(1,128)}, bf16[4608,128]{1,0:T(8,128)(2,1)}) custom-call(bf16[4608,128]{1,0:T(8,128)(2,1)} %bitcast.9, bf16[256,4608]{1,0:T(8,128)(2,1)} %get-tuple-element.11.scaled_ref, f32[384,384]{1,0:T(8,128)} %get-tuple-element.12.gram_ref, bf16[256,384]{1,0:T(8,128)(2,1)} %get-tuple-element.13.coords_ref), custom_call_target="tpu_custom_call" | custom-call | tf_op jit(solution)/shard_map/pallas_call | solution.py:144
  110.2 39.2 %shard_map.78 = bf16[288,2048]{1,0:T(8,128)(2,1)} custom-call(bf16[4608,128]{1,0:T(8,128)(2,1)} %get-tuple-element.16.update_ref), custom_call_target="tpu_custom_call" | custom-call | tf_op jit(solution)/shard_map/pallas_call | solution.py:213
  149.5 2.4 %copy.9 = bf16[288,2048]{1,0:T(8,128)(2,1)} copy(bf16[288,2048]{1,0:T(8,128)(2,1)} %shard_map.78) | data formatting | bytes 2359296

commit v5 on v4

--- a/solution.py
+++ b/solution.py
@@ -326,7 +326,7 @@
 
     def acts_second(part, shift):
         slot = shift + 3
-        up = slot % 2
+        up = part if shift in (0, 4) else int(shift > 0)
         for k, back in enumerate((3, 1)):
             piece = acts_piece(ring(y, back), shift).at[parts[part]]
             arrived(piece, y_recv.at[k, part, slot])
@@ -488,8 +488,6 @@
     acts_second(0, -2)
     cotan_third(0, 0)
     cotan_third(0, 1)
-    acts_second(1, 1)
-    acts_second(1, -1)
     cotan_second(1, 0)
     cotan_second(3, 0)
     cotan_second(1, 1)
@@ -498,6 +496,8 @@
     along_y(1, -2)
     acts_first(4)
     cotan_first(2, 0)
+    acts_second(1, 1)
+    acts_second(1, -1)
     acts_third(0, 0)
     acts_third(0, 1)
     acts_third(0, -1)
@@ -509,18 +509,20 @@
     cotan_third(3, 0)
     along_y(1, 3)
     along_y(1, -3)
+    cotan_first(2, 1)
+    cotan_second(2, 0)
     cotan_third(1, 1)
     cotan_third(3, 1)
-    cotan_first(2, 1)
-    cotan_second(2, 0)
     acts_second(0, 4)
+    cotan_second(2, 1)
     acts_second(1, 2)
     acts_second(1, -2)
+    cotan_third(2, 0)
     acts_third(1, 0)
     acts_third(1, 1)
     acts_third(1, -1)
     multiply(0, 1, True, False)
-    cotan_second(2, 1)
+    cotan_third(2, 1)
     acts_third(0, 2)
     acts_third(0, -2)
     acts_third(0, 3)
@@ -529,14 +531,12 @@
     multiply(1, 0, False, False)
     cotan_last(3)
     multiply(3, 0, False, False)
-    cotan_third(2, 0)
     acts_second(1, 3)
     acts_second(1, -3)
+    acts_second(1, 4)
     acts_third(0, 4)
-    cotan_third(2, 1)
     cotan_last(2)
     multiply(2, 0, False, True)
-    acts_second(1, 4)
     acts_third(1, 2)
     acts_third(1, -2)
     acts_third(1, 3)

time: 153 us -> 149 us (0.974)
  the two profiles are of different devices: /device:TPU:26 before, /device:TPU:92 now
where the time goes in v5:
time: 149 us
  Pallas kernels  146 us (98%)
  local copies, waits for them, and re-layouts  2.41 us (2%)
    pallas_call x1, Pallas kernels, gradient(): pl.pallas_call(gradient_kernel, out_shape=(jax.ShapeDtypeStruct((2, 8, fe...  79.7 us
    pallas_call x1, Pallas kernels, exchange(): pl.pallas_call(functools.partial(exchange_kernel, shares), out_shape=jax....  37.8 us
    pallas_call x1, Pallas kernels, sketch(): pl.pallas_call(sketch_kernel, grid=(depth // block,), out_shape=(jax.Shap...  28.5 us

profile of v5, /device:TPU:92, one launch (start us, length us, event | category | flops | bytes accessed | tf_op | source)
XLA Modules:
  0.0 149.0 jit_solution(16634170513039245374)
XLA Ops:
  0.6 79.7 %shard_map.76 = (bf16[2,8,288,128]{3,2,1,0:T(8,128)(2,1)}, bf16[256,4608]{1,0:T(8,128)(2,1)}, f32[384,384]{1,0:T(8,128)}, bf16[256,384]{1,0:T(8,128)(2,1)}) custom-call(bf16[288,256]{1,0:T(8,128)(2,1)} %bitcast.10, bf16[256,2048]{1,0:T(8,128)(2,1)} %cotan_ref.1, bf16[256,4608]{1,0:T(8,128)(2,1)} %bitcast.7, f32[1,256]{1,0:T(1,128)} %bitcast.11, ...), custom_call_target="tpu_custom_call" | custom-call | tf_op jit(solution)/shard_map/pallas_call | solution.py:588
  80.3 28.5 %shard_map.77 = (bf16[256,4608]{1,0:T(8,128)(2,1)}, f32[1,256]{1,0:T(1,128)}, bf16[4608,128]{1,0:T(8,128)(2,1)}) custom-call(bf16[4608,128]{1,0:T(8,128)(2,1)} %bitcast.9, bf16[256,4608]{1,0:T(8,128)(2,1)} %get-tuple-element.11.scaled_ref, f32[384,384]{1,0:T(8,128)} %get-tuple-element.12.gram_ref, bf16[256,384]{1,0:T(8,128)(2,1)} %get-tuple-element.13.coords_ref), custom_call_target="tpu_custom_call" | custom-call | tf_op jit(solution)/shard_map/pallas_call | solution.py:144
  108.8 37.8 %shard_map.78 = bf16[288,2048]{1,0:T(8,128)(2,1)} custom-call(bf16[4608,128]{1,0:T(8,128)(2,1)} %get-tuple-element.16.update_ref), custom_call_target="tpu_custom_call" | custom-call | tf_op jit(solution)/shard_map/pallas_call | solution.py:213
  146.6 2.4 %copy.9 = bf16[288,2048]{1,0:T(8,128)(2,1)} copy(bf16[288,2048]{1,0:T(8,128)(2,1)} %shard_map.78) | data formatting | bytes 2359296
